TPU v7x, 128 devices: a whole 4x4x4 slice. The times are simulated.
128 devices in a mesh: rep: 8 (over z_lo, x), tp: 16 (over z_hi, y, core).
Axes of the slice: x: 4, y: 4, z: 4 (z_hi: 2, z_lo: 2; z = z_hi * 2 + z_lo), core: 2. Of those that a mesh axis runs over, the one named last changes fastest.
Arguments:
- step_token_index: int32 [4, 1024], replicated, may hold values from 0 to 75967
- row_tenant_index: int32 [1024], P('rep'), may hold values from 0 to 3
- stored_lengths: int32 [1024], P('rep'), may hold values from 1 to 192, as said below
- embedding: bfloat16 [75968, 5120], P('rep', 'tp'), may hold values from -6 to 6
- input_norm_gain: float32 [5120], replicated, may hold values from 0.1 to 1.9
- query_weight: bfloat16 [5120, 8192], P(None, 'tp'), may hold values from -0.078125 to 0.078125
- key_weight: bfloat16 [5120, 1024], P(None, 'tp'), may hold values from -0.078125 to 0.078125
- value_weight: bfloat16 [5120, 1024], P(None, 'tp'), may hold values from -0.078125 to 0.078125
- output_weight: bfloat16 [8192, 5120], P('tp'), may hold values from -0.0625 to 0.0625
- query_norm_gain: float32 [128], replicated, may hold values from 0.1 to 1.9
- key_norm_gain: float32 [128], replicated, may hold values from 0.1 to 1.9
- adapter_down_weight: bfloat16 [4, 5120, 128], P(None, 'tp', 'rep'), may hold values from -0.078125 to 0.078125
- adapter_up_weight: bfloat16 [4, 128, 8192], P(None, 'rep', 'tp'), may hold values from -0.5 to 0.5
- stored_keys: bfloat16 [1024, 1536, 128], P('rep', 'tp'), may hold values from -360 to 360
- stored_values: bfloat16 [1024, 1536, 128], P('rep', 'tp'), may hold values from -6 to 6
Outputs:
- layer_out: bfloat16 [4, 1024, 5120], P(None, 'rep', 'tp')
Inputs may be any that keep to these rules, and one draw needn't show every extreme that they name: `stored_lengths`: some row of every draw has 192 cached positions and some row has 1.
All inputs are finite; a program needn't handle non-finite values.
Results may differ from a plain program's by a relative error of at most 0.015.
Values may be sent and summed in bfloat16 or wider, within the bound.
No kernel may reach another device: no remote copies, remote signals or barrier semaphores. Data moves between devices by JAX's collectives and lax.ppermute only.
A program may use at most 256 MiB of HBM per device.

v0:
```python
import jax
import jax.numpy as jnp
from jax import lax
from jax.sharding import PartitionSpec as P

epsilon = 1e-06
rope_base = 1000000.0
adapter_scale = 2.0
masked_score = -1e30


def from_partner(block, axis, distance):
    count = lax.axis_size(axis)
    route = []
    for low in range(count):
        high = low | 1 << distance
        if high != low and high < count:
            route += [(low, high), (high, low)]
    return lax.ppermute(block, axis, route)


def rms_scale(vector, gain):
    power = jnp.mean(vector * vector, axis=-1, keepdims=True)
    return vector * lax.rsqrt(power + epsilon) * gain


def rotary(vector, position):
    half_dim = vector.shape[-1] // 2
    inverse = rope_base ** (-jnp.arange(half_dim, dtype=jnp.float32) / half_dim)
    angle = position.astype(jnp.float32)[..., None] * inverse
    cosine = jnp.cos(angle)
    sine = jnp.sin(angle)
    first = vector[..., :half_dim]
    second = vector[..., half_dim:]
    return jnp.concatenate(
        [first * cosine - second * sine, second * cosine + first * sine], axis=-1
    )


def attend_block(
    query_heads, key_block, value_block, first_position, new_keys, new_values, lengths, take_new
):
    step_count = query_heads.shape[0]
    score_scale = query_heads.shape[-1] ** (-0.5)
    cached = (
        jnp.einsum("srhd,rpd->srhp", query_heads, key_block, preferred_element_type=jnp.float32)
        * score_scale
    )
    position = first_position + jnp.arange(key_block.shape[1])
    valid = position[None, :] < lengths[:, None]
    cached = jnp.where(valid[None, :, None, :], cached, masked_score)
    fresh = (
        jnp.einsum("srhd,trd->srht", query_heads, new_keys, preferred_element_type=jnp.float32)
        * score_scale
    )
    order = jnp.arange(step_count)
    causal = jnp.logical_and(order[None, :] <= order[:, None], take_new)
    fresh = jnp.where(causal[:, None, None, :], fresh, masked_score)
    peak = jnp.maximum(jnp.max(cached, axis=-1), jnp.max(fresh, axis=-1))
    cached_weight = jnp.exp(cached - peak[..., None])
    fresh_weight = jnp.exp(fresh - peak[..., None])
    total = jnp.sum(cached_weight, axis=-1) + jnp.sum(fresh_weight, axis=-1)
    weighted = jnp.einsum(
        "srhp,rpd->srhd", cached_weight, value_block, preferred_element_type=jnp.float32
    )
    weighted = weighted + jnp.einsum(
        "srht,trd->srhd", fresh_weight, new_values, preferred_element_type=jnp.float32
    )
    return (peak, total, weighted)


def merge_partials(peak_one, total_one, weighted_one, peak_two, total_two, weighted_two):
    peak = jnp.maximum(peak_one, peak_two)
    factor_one = jnp.exp(peak_one - peak)
    factor_two = jnp.exp(peak_two - peak)
    total = total_one * factor_one + total_two * factor_two
    weighted = weighted_one * factor_one[..., None] + weighted_two * factor_two[..., None]
    return (peak, total, weighted)


def on_device(
    step_token_index,
    row_tenant_index,
    stored_lengths,
    embedding,
    input_norm_gain,
    query_weight,
    key_weight,
    value_weight,
    output_weight,
    query_norm_gain,
    key_norm_gain,
    adapter_down_weight,
    adapter_up_weight,
    stored_keys,
    stored_values,
):
    step_count = step_token_index.shape[0]
    row_count = row_tenant_index.shape[0]
    total_rows = step_count * row_count
    head_size = query_norm_gain.shape[0]
    vocab_rows = embedding.shape[0]
    first_id = lax.axis_index("rep") * vocab_rows
    local_ids = step_token_index - first_id
    inside = jnp.logical_and(local_ids >= 0, local_ids < vocab_rows)
    picked = jnp.take(embedding, jnp.clip(local_ids, 0, vocab_rows - 1), axis=0)
    lookup = jnp.where(inside[..., None], picked.astype(jnp.float32), 0.0)
    own_cols = lax.psum_scatter(lookup.astype(jnp.bfloat16), "rep", scatter_dimension=1, tiled=True)
    gathered = lax.all_gather(own_cols, "tp", axis=2, tiled=True)
    normalized_input = rms_scale(gathered.astype(jnp.float32), input_norm_gain).astype(jnp.bfloat16)
    normed_rows = normalized_input.reshape(total_rows, gathered.shape[2])
    down_local, up_local = (
        lax.all_gather(adapter_down_weight, "rep", axis=2, tiled=True),
        lax.all_gather(adapter_up_weight, "rep", axis=1, tiled=True),
    )
    tenant_count = down_local.shape[0]
    rank_size = down_local.shape[2]
    tenant_rows = jnp.tile(row_tenant_index, step_count)
    tenant_picker = (tenant_rows[:, None] == jnp.arange(tenant_count)[None, :]).astype(jnp.float32)
    down_full = lax.all_gather(down_local, "tp", axis=1, tiled=True)
    per_tenant = jnp.einsum(
        "nd,edr->ner", normed_rows, down_full, preferred_element_type=jnp.float32
    )
    reduced_rank_rows = jnp.sum(per_tenant * tenant_picker[:, :, None], axis=1)
    reduced_rank_rows = reduced_rank_rows.astype(jnp.bfloat16)
    spread = (
        reduced_rank_rows[:, None, :] * tenant_picker.astype(jnp.bfloat16)[:, :, None]
    ).reshape(total_rows, tenant_count * rank_size)
    up_rows = up_local.reshape(tenant_count * rank_size, up_local.shape[2])
    query_projected = jnp.dot(normed_rows, query_weight, preferred_element_type=jnp.float32)
    query_projected = query_projected + adapter_scale * jnp.dot(
        spread, up_rows, preferred_element_type=jnp.float32
    )
    heads = query_weight.shape[1] // head_size
    positions = jnp.tile(stored_lengths, step_count) + jnp.repeat(jnp.arange(step_count), row_count)
    queries = rotary(
        rms_scale(query_projected.reshape(total_rows, heads, head_size), query_norm_gain),
        positions[:, None],
    )
    queries = queries.astype(jnp.bfloat16).reshape(step_count, row_count, heads, head_size)
    key_half = jnp.dot(normed_rows, key_weight, preferred_element_type=jnp.float32).astype(
        jnp.bfloat16
    )
    value_half = jnp.dot(normed_rows, value_weight, preferred_element_type=jnp.float32).astype(
        jnp.bfloat16
    )
    parity = lax.axis_index("tp") % 2
    other_key, other_value = from_partner((key_half, value_half), "tp", 0)
    low_first = parity == 0
    full_key = jnp.where(
        low_first,
        jnp.concatenate([key_half, other_key], axis=1),
        jnp.concatenate([other_key, key_half], axis=1),
    )
    full_value = jnp.where(
        low_first,
        jnp.concatenate([value_half, other_value], axis=1),
        jnp.concatenate([other_value, value_half], axis=1),
    )
    key_wide = lax.optimization_barrier(full_key).astype(jnp.float32)
    keys_new = (
        rotary(rms_scale(key_wide, key_norm_gain), positions)
        .astype(jnp.bfloat16)
        .reshape(step_count, row_count, head_size)
    )
    values_new = full_value.reshape(step_count, row_count, head_size)
    block_size = stored_keys.shape[1]
    other_keys, other_values = from_partner((stored_keys, stored_values), "tp", 0)
    peak_own, total_own, weighted_own = attend_block(
        queries,
        stored_keys,
        stored_values,
        parity * block_size,
        keys_new,
        values_new,
        stored_lengths,
        parity == 0,
    )
    peak_far, total_far, weighted_far = attend_block(
        queries,
        other_keys,
        other_values,
        (1 - parity) * block_size,
        keys_new,
        values_new,
        stored_lengths,
        parity == 1,
    )
    peak, total, weighted = merge_partials(
        peak_own, total_own, weighted_own, peak_far, total_far, weighted_far
    )
    attended = (
        (weighted / total[..., None]).astype(jnp.bfloat16).reshape(total_rows, heads * head_size)
    )
    column_count = output_weight.shape[1] // lax.axis_size("tp")
    summed = lax.psum_scatter(
        lax.dot_general(
            output_weight, attended, (((0,), (1,)), ((), ())), preferred_element_type=jnp.float32
        ),
        "tp",
        scatter_dimension=0,
        tiled=True,
    )
    residual_rows = own_cols.reshape(total_rows, column_count).astype(jnp.float32)
    result = (residual_rows + summed.T).astype(jnp.bfloat16)
    return result.reshape(step_count, row_count, column_count)


def solution(mesh):
    return jax.shard_map(
        on_device,
        mesh=mesh,
        in_specs=(
            P(),
            P("rep"),
            P("rep"),
            P("rep", "tp"),
            P(),
            P(None, "tp"),
            P(None, "tp"),
            P(None, "tp"),
            P("tp", None),
            P(),
            P(),
            P(None, "tp", "rep"),
            P(None, "rep", "tp"),
            P("rep", "tp", None),
            P("rep", "tp", None),
        ),
        out_specs=P(None, "rep", "tp"),
        check_vma=False,
    )
```

profile of v0, /device:TPU:1, one launch (start us, length us, event | category | flops | bytes accessed | tf_op | source)
XLA Modules:
  0.0 651.4 jit_solution(386451906222661027)
XLA Ops:
  8.1 9.6 %copy.59 = bf16[9496,320]{1,0:T(8,128)(2,1)} copy(bf16[9496,320]{0,1:T(8,128)(2,1)} %param.18) | data formatting | bytes 12154880 | tf_op args[3]
  17.7 20.7 %gather_fusion = bf16[4096,320]{1,0:T(8,128)(2,1)} fusion(bf16[9496,320]{1,0:T(8,128)(2,1)} %copy.59, s32[4096]{0:T(1024)S(1)} %bitcast_clamp_fusion), kind=kCustom, calls=%fused_computation | custom fusion | bytes 5259264 | tf_op jit(solution)/shard_map/jit(_take)/gather | solution.py:106
  38.5 5.0 copy.60
  43.5 2.9 select_convert_fusion
  46.4 57.6 %copy.89 = bf16[4,1024,320]{0,2,1:T(8,128)(2,1)} copy(bf16[4,1024,320]{1,0,2:T(4,128)(2,1)} %select_convert_fusion) | data formatting | bytes 5242880
  104.0 163.1 %reshape.367 = bf16[1024,1280]{1,0:T(8,128)(2,1)} reshape(bf16[1024,320,4]{2,1,0:T(8,128)(2,1)} %bitcast.31) | data formatting | bytes 5242880
  267.2 43.3 %reduce-scatter.7.cloned.1.call-done = bf16[128,1280]{1,0:T(8,128)(2,1)} async-done(((bf16[1024,1280]{1,0:T(8,128)(2,1)}), bf16[128,1280]{1,0:T(8,128)(2,1)}) %reduce-scatter.7.cloned.1.call-update) | async-done | bytes 327696
  310.5 24.3 %reshape.368 = bf16[128,320,4]{2,1,0:T(8,128)(2,1)} reshape(bf16[128,1280]{1,0:T(8,128)(2,1)} %reduce-scatter.7.cloned.1.call-done) | data formatting | bytes 655360
  334.8 10.4 %copy.90 = bf16[4,128,320]{1,0,2:T(4,128)(2,1)} copy(bf16[4,128,320]{0,2,1:T(8,128)(2,1)} %bitcast.184) | data formatting | bytes 655360
  345.4 22.7 %all_gather.13 = bf16[4,320,128]{1,0,2:T(4,128)(2,1)S(1)} all-gather(bf16[4,320,16]{1,0,2:T(4,128)(2,1)S(1)} %copy.61), channel_id=1, replica_groups=mesh['rep'=8,'tp'=16] {'rep'}, dimensions={2}, use_global_device_ids=true | all-gather | bytes 368640 | tf_op jit(solution)/shard_map/all_gather | solution.py:113
  369.2 11.5 %collective-permute-start.2 = (bf16[128,96,128]{2,1,0:T(8,128)(2,1)}, bf16[128,96,128]{2,1,0:T(8,128)(2,1)}, u32[]{:S(2)}, u32[]{:S(2)}) collective-permute-start(bf16[128,96,128]{2,1,0:T(8,128)(2,1)} %param.28), channel_id=1, source_target_pairs={{0,1},{1,0},{2,3},{3,2},{4,5},{5,4},{6,7},{7,6},{8,9},{9,8},{10,11... | collective-permute-start | bytes 9437192 | tf_op jit(solution)/shard_map/ppermute | solution.py:19
  381.0 24.9 %all_gather.15 = bf16[4,128,512]{2,1,0:T(8,128)(2,1)S(1)} all-gather(bf16[4,16,512]{2,1,0:T(8,128)(2,1)S(1)} %copy-done.7), channel_id=1, replica_groups=mesh['rep'=8,'tp'=16] {'rep'}, dimensions={1}, use_global_device_ids=true | all-gather | bytes 589824 | tf_op jit(solution)/shard_map/all_gather | solution.py:114
  405.8 6.6 %all-gather.3.cloned.1.call-done = bf16[4,128,5120]{1,0,2:T(4,128)(2,1)} async-done(((bf16[4,128,320]{1,0,2:T(4,128)(2,1)}), bf16[4,128,5120]{1,0,2:T(4,128)(2,1)}) %all-gather.3.cloned.1.call-update) | async-done | bytes 5242896 | tf_op jit(solution)/shard_map/all_gather | solution.py:109
  412.4 7.1 %fusion = f32[4,128]{1,0:T(4,128)S(1)} fusion(bf16[4,128,5120]{1,0,2:T(4,128)(2,1)} %all-gather.3.cloned.1.call-done), kind=kLoop, calls=%fused_computation.3 | loop fusion | flops 7863808 | bytes 5244928 | tf_op jit(solution)/shard_map/reduce_sum | solution.py:23
  419.6 14.7 %fusion.2 = bf16[4,128,5120]{1,0,2:T(4,128)(2,1)S(1)} fusion(bf16[4,128,5120]{1,0,2:T(4,128)(2,1)S(1)} %copy-done.2, f32[5120]{0:T(1024)S(1)} %copy-done.9, f32[4,128]{1,0:T(4,128)S(1)} %add_rsqrt_fusion.2), kind=kLoop, calls=%fused_computation.5 | loop fusion | flops 10485760 | bytes 10508288 | tf_op jit(solution)/shard_map/convert_element_type | solution.py:110
  437.2 36.7 %all-gather.5.cloned.1.call-done = bf16[4,5120,128]{2,0,1:T(4,128)(2,1)} async-done(((bf16[4,320,128]{2,0,1:T(4,128)(2,1)}), bf16[4,5120,128]{2,0,1:T(4,128)(2,1)}) %all-gather.5.cloned.1.call-update) | async-done | bytes 5242896 | tf_op jit(solution)/shard_map/all_gather | solution.py:120
  473.9 7.1 %fusion.68 = bf16[512,128]{1,0:T(8,128)(2,1)S(1)} fusion(bf16[4,5120,128]{2,0,1:T(4,128)(2,1)} %all-gather.5.cloned.1.call-done, bf16[640,8,4,128]{3,2,1,0:T(4,128)(2,1)} %bitcast.190, f32[512,4]{0,1:T(4,128)S(1)} %get-tuple-element.22), kind=kOutput, calls=%fused_computation.50 | convolution fusion | flops 2684813312 | bytes 10625024 | tf_op jit(solution)/shard_map/nd,edr->ner/dot_general | solution.py:121
  481.1 4.9 fusion.7
  491.3 5.3 select_reduce_fusion
  496.6 4.1 fusion.121
  512.0 3.3 fusion.80
  515.6 5.4 convolution_bitcast_fusion
  521.0 11.4 %copy.91 = f32[5120,512]{1,0:T(8,128)} copy(f32[5120,512]{0,1:T(8,128)} %convolution_bitcast_fusion) | data formatting | bytes 20971520
  533.6 108.7 %reduce-scatter.9.cloned.1.call-done = f32[320,512]{1,0:T(8,128)} async-done(((f32[5120,512]{1,0:T(8,128)}), f32[320,512]{1,0:T(8,128)}) %reduce-scatter.9.cloned.1.call-update) | async-done | bytes 655376
  (104 shorter events, 26.1 us)
Async XLA Ops:
  6.5 427.8 %copy-start = (bf16[5120,64]{0,1:T(8,128)(2,1)S(1)}, bf16[5120,64]{0,1:T(8,128)(2,1)}, u32[]{:S(2)}) copy-start(bf16[5120,64]{0,1:T(8,128)(2,1)} %param.21) | copy-start | bytes 1966084
  6.5 303.9 %reduce-scatter.7.cloned.1.call-start = ((), (), s32[]{:S(2)}) async-start(), calls=%async_computation.4 | async-start | bytes 2949120
  267.1 145.3 %all-gather.3.cloned.1.call-start = ((), (), s32[]{:S(2)}) async-start(), calls=%async_computation.2 | async-start | bytes 5570560 | tf_op jit(solution)/shard_map/all_gather | solution.py:109
  334.8 10.5 %copy-start.8 = (bf16[4,320,16]{1,2,0:T(8,128)(2,1)S(1)}, bf16[4,320,16]{1,2,0:T(8,128)(2,1)}, u32[]{:S(2)}) copy-start(bf16[4,320,16]{1,2,0:T(8,128)(2,1)} %param.26) | copy-start | bytes 122884
  334.8 46.0 %copy-start.10 = (s32[128]{0:T(128)S(1)}, s32[128]{0:T(128)}, u32[]{:S(2)}) copy-start(s32[128]{0:T(128)} %param.17) | copy-start | bytes 1540
  334.8 46.0 %copy-start.13 = (s32[128]{0:T(128)S(1)}, s32[128]{0:T(128)}, u32[]{:S(2)}) copy-start(s32[128]{0:T(128)} %param.16) | copy-start | bytes 1540
  334.8 46.2 %copy-start.7 = (bf16[4,16,512]{2,1,0:T(8,128)(2,1)S(1)}, bf16[4,16,512]{2,1,0:T(8,128)(2,1)}, u32[]{:S(2)}) copy-start(bf16[4,16,512]{2,1,0:T(8,128)(2,1)} %param.27) | copy-start | bytes 196612
  345.2 74.3 %copy-start.9 = (f32[5120]{0:T(1024)S(1)}, f32[5120]{0:T(1024)}, u32[]{:S(2)}) copy-start(f32[5120]{0:T(1024)} %param.19) | copy-start | bytes 61444
  345.3 128.7 %all-gather.5.cloned.1.call-start = ((), (), s32[]{:S(2)}) async-start(), calls=%async_computation.3 | async-start | bytes 5570560 | tf_op jit(solution)/shard_map/all_gather | solution.py:120
  369.1 273.1 %reduce-scatter.9.cloned.1.call-start = ((), (), s32[]{:S(2)}) async-start(), calls=%async_computation.5 | async-start | bytes 11141120
  369.2 127.4 %collective-permute-start.2 = (bf16[128,96,128]{2,1,0:T(8,128)(2,1)}, bf16[128,96,128]{2,1,0:T(8,128)(2,1)}, u32[]{:S(2)}, u32[]{:S(2)}) collective-permute-start(bf16[128,96,128]{2,1,0:T(8,128)(2,1)} %param.28), channel_id=1, source_target_pairs={{0,1},{1,0},{2,3},{3,2},{4,5},{5,4},{6,7},{7,6},{8,9},{9,8},{10,11... | collective-permute-start | bytes 9437192 | tf_op jit(solution)/shard_map/ppermute | solution.py:19
  380.7 131.3 %collective-permute-start.3 = (bf16[128,96,128]{2,1,0:T(8,128)(2,1)}, bf16[128,96,128]{2,1,0:T(8,128)(2,1)}, u32[]{:S(2)}, u32[]{:S(2)}) collective-permute-start(bf16[128,96,128]{2,1,0:T(8,128)(2,1)} %param.29), channel_id=1, source_target_pairs={{0,1},{1,0},{2,3},{3,2},{4,5},{5,4},{6,7},{7,6},{8,9},{9,8},{10,11... | collective-permute-start | bytes 9437192 | tf_op jit(solution)/shard_map/ppermute | solution.py:19
  412.4 7.1 %copy-start.2 = (bf16[4,128,5120]{1,0,2:T(4,128)(2,1)S(1)}, bf16[4,128,5120]{1,0,2:T(4,128)(2,1)}, u32[]{:S(2)}) copy-start(bf16[4,128,5120]{1,0,2:T(4,128)(2,1)} %all-gather.3.cloned.1.call-done) | copy-start | bytes 15728644
  434.3 2.6 copy-start.3
  435.3 53.3 %collective-permute-start = (bf16[512,64]{0,1:T(8,128)(2,1)S(1)}, bf16[512,64]{0,1:T(8,128)(2,1)S(1)}, u32[]{:S(2)}, u32[]{:S(2)}) collective-permute-start(bf16[512,64]{0,1:T(8,128)(2,1)S(1)} %fusion.74), channel_id=1, source_target_pairs={{0,1},{1,0},{2,3},{3,2},{4,5},{5,4},{6,7},{7,6},{8,9},{9,8},{10,11... | collective-permute-start | bytes 196616 | tf_op jit(solution)/shard_map/ppermute | solution.py:19
  436.9 54.2 %collective-permute-start.1 = (bf16[512,64]{0,1:T(8,128)(2,1)S(1)}, bf16[512,64]{0,1:T(8,128)(2,1)S(1)}, u32[]{:S(2)}, u32[]{:S(2)}) collective-permute-start(bf16[512,64]{0,1:T(8,128)(2,1)S(1)} %fusion.71), channel_id=1, source_target_pairs={{0,1},{1,0},{2,3},{3,2},{4,5},{5,4},{6,7},{7,6},{8,9},{9,8},{10,11... | collective-permute-start | bytes 196616 | tf_op jit(solution)/shard_map/ppermute | solution.py:19
  473.9 7.1 %copy-start.4 = (bf16[4,128,5120]{1,0,2:T(4,128)(2,1)S(1)}, bf16[4,128,5120]{1,0,2:T(4,128)(2,1)}, u32[]{:S(2)}) copy-start(bf16[4,128,5120]{1,0,2:T(4,128)(2,1)} %copy-done.3) | copy-start | bytes 15728644
  481.0 7.2 %copy-start.11 = (f32[128]{0:T(128)S(1)}, f32[128]{0:T(128)}, u32[]{:S(2)}) copy-start(f32[128]{0:T(128)} %param.24) | copy-start | bytes 1540
  486.0 2.8 copy-start.12
  491.3 9.5 %copy-start.5 = (bf16[128,96,128]{2,1,0:T(8,128)(2,1)S(1)}, bf16[128,96,128]{2,1,0:T(8,128)(2,1)}, u32[]{:S(2)}) copy-start(bf16[128,96,128]{2,1,0:T(8,128)(2,1)} %param.28) | copy-start | bytes 9437188
  506.7 3.7 copy-start.14
  510.4 5.1 slice-start
  512.0 3.6 slice-start.1
  533.4 111.2 %copy-start.1 = (bf16[5120,64]{0,1:T(8,128)(2,1)S(1)}, bf16[5120,64]{0,1:T(8,128)(2,1)}, u32[]{:S(2)}) copy-start(bf16[5120,64]{0,1:T(8,128)(2,1)} %param.21) | copy-start | bytes 1966084
  (2 other events, 2.5 us)
Sparse Core Ops, SparseCore 0:
  267.2 43.1 reduce-scatter.6
  345.4 67.0 all-gather.2
  414.9 58.9 all-gather.4
  532.5 109.6 reduce-scatter.8
where the time goes:
time: 663 us; the launch traced here: 651 us
  local copies, waits for them, and re-layouts  309 us (47%)
  waiting for transfers between devices  195 us (29%)
  blocking collectives  47.6 us (7%)
  matrix products  40.5 us (6%)
  other arithmetic  32.8 us (5%)
  between operations  13.9 us (2%)
  starting transfers between devices  12.4 us (2%)
    unnamed x44, local copies, waits for them, and re-layouts  279 us
    unnamed x6, waiting for transfers between devices  152 us
    all_gather x1, waiting for transfers between devices, on_device(): down_full = lax.all_gather(down_local, 'tp', axis=1, tiled=True)  36.7 us
    gather x2, local copies, waits for them, and re-layouts, on_device(): picked = jnp.take(embedding, jnp.clip(local_ids, 0, vocab_rows - 1), axis=0)  25.7 us
    all_gather x1, blocking collectives, on_device(): lax.all_gather(adapter_up_weight, 'rep', axis=1, tiled=True)  24.9 us
    all_gather x1, blocking collectives, on_device(): lax.all_gather(adapter_down_weight, 'rep', axis=2, tiled=True)  22.7 us
    convert_element_type x1, other arithmetic, on_device(): rms_scale(gathered.astype(jnp.float32), input_norm_gain)  14.7 us
  transfers between devices with their start and end apart: 8, of which 4 were waited for; matrix products, arithmetic and copies ran while one was open for 10% of the time, Pallas kernels for 0%

commit v1 on v0

v1 whole, which is shorter than its diff:
```python
import jax
import jax.numpy as jnp
import numpy as np
from jax import lax
from jax.experimental import pallas as pl
from jax.experimental.pallas import tpu as pltpu
from jax.sharding import PartitionSpec as P

epsilon = 1e-06
rope_base = 1000000.0
adapter_scale = 2.0
masked_score = -1e30
slots = 128


def tp_route(dz, dy, dc):
    route = []
    for place in range(16):
        z, y, core = place // 8, place // 2 % 4, place % 2
        route.append((place, (z + dz) % 2 * 8 + (y + dy) % 4 * 2 + (core + dc) % 2))
    return route


def rep_route(dz, dx):
    return [(place, (place // 4 + dz) % 2 * 4 + (place + dx) % 4) for place in range(8)]


def to_tp(block, dz, dy):
    return lax.ppermute(block, "tp", tp_route(dz, dy, 0))


def to_partner(block):
    return lax.ppermute(block, "tp", tp_route(0, 0, 1))


def over_replicas(block):
    count = lax.axis_size("rep")
    copies = jnp.broadcast_to(block[None], (count, *block.shape))
    return lax.all_to_all(copies, "rep", 0, 0, tiled=True)


def rope_tables(positions, half_dim):
    inverse = rope_base ** (-jnp.arange(half_dim, dtype=jnp.float32) / half_dim)
    angle = positions.astype(jnp.float32)[:, None] * inverse
    return jnp.cos(angle), jnp.sin(angle)


f32 = jnp.float32
bf16 = jnp.bfloat16
i32 = jnp.int32
megabyte = 1 << 20


def shape_of(shape, dtype):
    return jax.ShapeDtypeStruct(shape, dtype)


def nn(left, right):
    return jnp.dot(left, right, preferred_element_type=f32)


def nt(left, right):
    return lax.dot_general(left, right, (((1,), (1,)), ((), ())), preferred_element_type=f32)


def whole(array):
    return pl.BlockSpec(array.shape, lambda *_: (0,) * len(array.shape))


def call(kernel, out_shape, operands, scalars=(), grid=(1,), in_specs=None, out_specs=None, **extra):
    if in_specs is None:
        in_specs = [None] * len(operands)
    in_specs = [spec or whole(operand) for spec, operand in zip(in_specs, operands)]
    if out_specs is None:
        out_specs = jax.tree.map(whole, out_shape)
    flops = extra.pop("flops", 1 << 20)
    scratch = extra.pop("scratch", [])
    room = extra.pop("room", 8)
    moved = sum(operand.size * operand.dtype.itemsize for operand in operands)
    return pl.pallas_call(
        kernel,
        out_shape=out_shape,
        grid_spec=pltpu.PrefetchScalarGridSpec(
            num_scalar_prefetch=len(scalars),
            grid=grid,
            in_specs=in_specs,
            out_specs=out_specs,
            scratch_shapes=scratch,
        ),
        compiler_params=pltpu.CompilerParams(vmem_limit_bytes=room * megabyte),
        cost_estimate=pl.CostEstimate(flops=flops, bytes_accessed=moved, transcendentals=0),
    )(*scalars, *operands)


def after(value, *others):
    def kernel(*refs):
        del refs

    anywhere = pl.BlockSpec(memory_space=pl.ANY)
    return pl.pallas_call(
        kernel,
        out_shape=shape_of(value.shape, value.dtype),
        in_specs=[anywhere] * (1 + len(others)),
        out_specs=anywhere,
        input_output_aliases={0: 0},
    )(value, *others)


def ranks(tokens, me, vocab_rows):
    parts, count = tokens.shape

    def kernel(me_ref, tokens_ref, rank_ref, most_ref):
        owner = tokens_ref[...] // vocab_rows
        own = tokens_ref[pl.ds(me_ref[0], 1), :] // vocab_rows
        from_part = lax.broadcasted_iota(i32, (parts, count), 0) == own
        wanted = jnp.concatenate([(owner == me_ref[0]).astype(f32), from_part.astype(f32)], axis=0)
        earlier = lax.broadcasted_iota(i32, (count, count), 0) < lax.broadcasted_iota(
            i32, (count, count), 1
        )
        rank = nn(wanted.astype(bf16), earlier.astype(f32).astype(bf16)).astype(i32)
        rank_ref[...] = jnp.where(wanted > 0, rank, -1)
        most = jnp.zeros((parts, 1), f32)
        for part in range(parts):
            found = jnp.sum((owner == part).astype(f32), axis=1, keepdims=True)
            most = jnp.maximum(most, found)
        most_ref[0] = jnp.max(most).astype(i32)

    return call(
        kernel,
        (shape_of((2 * parts, count), i32), shape_of((1,), i32)),
        (tokens,),
        scalars=(me.reshape(1),),
        out_specs=(
            whole(shape_of((2 * parts, count), i32)),
            pl.BlockSpec(memory_space=pltpu.SMEM),
        ),
    )


def pick(tokens, rank, table, me, base):
    parts, count = tokens.shape
    features, vocab_rows = table.shape
    tile, piece = 1280, 256
    steps = pl.cdiv(vocab_rows, tile)

    def kernel(me_ref, base_ref, tokens_ref, rank_ref, table_ref, out_ref, list_ref, total_ref):
        step = pl.program_id(0)

        @pl.when(step == 0)
        def _():
            place = base_ref[0] + lax.broadcasted_iota(i32, (slots, count), 0)
            for part in range(parts):
                local = tokens_ref[part : part + 1, :] - me_ref[0] * vocab_rows
                hit = (rank_ref[part : part + 1, :] == place).astype(f32).astype(bf16)
                inside = jnp.logical_and(local >= 0, local < vocab_rows)
                local = jnp.where(inside, local, 0)
                high = local // 128
                digits = jnp.concatenate(
                    [high, local - high * 128, jnp.ones((6, count), i32)], axis=0
                )
                found = nt(digits.astype(f32).astype(bf16), hit).astype(i32)
                name = found[0:1] * 128 + found[1:2]
                list_ref[part : part + 1, :] = jnp.where(found[2:3] > 0, name, -1)
            total_ref[...] = jnp.zeros_like(total_ref)

        def add(block):
            name = lax.broadcasted_iota(i32, (piece, slots), 0).astype(f32).astype(bf16)
            yes, no = jnp.ones((), bf16), jnp.zeros((), bf16)
            for part in range(0, parts, 2):
                chosen = []
                for side in (part, part + 1):
                    rows = []
                    for start in range(0, tile, piece):
                        wanted = list_ref[side : side + 1, :] - (step * tile + start)
                        wanted = jnp.clip(wanted, -1, piece).astype(f32).astype(bf16)
                        rows.append(jnp.where(name == wanted, yes, no))
                    chosen.append(jnp.concatenate(rows, axis=0))
                total_ref[:, part * slots : (part + 2) * slots] += nn(
                    block, jnp.concatenate(chosen, axis=1)
                )

        @pl.when(step < steps - 1)
        def _():
            add(table_ref[...])

        @pl.when(step == steps - 1)
        def _():
            lane = step * tile + lax.broadcasted_iota(i32, (1, tile), 1)
            add(jnp.where(lane < vocab_rows, table_ref[...].astype(f32), 0.0).astype(bf16))

        @pl.when(step == steps - 1)
        def _():
            for part in range(parts):
                out_ref[part] = total_ref[:, part * slots : (part + 1) * slots].astype(bf16)

    return call(
        kernel,
        shape_of((parts, features, slots), bf16),
        (tokens, rank, table),
        scalars=(me.reshape(1), base.reshape(1)),
        grid=(steps,),
        in_specs=[None, None, pl.BlockSpec((features, tile), lambda step, *_: (0, step))],
        scratch=[pltpu.VMEM((parts, slots), i32), pltpu.VMEM((features, parts * slots), f32)],
        flops=2 * features * vocab_rows * parts * slots,
        room=20,
    )


def place_slots(rank, got, base, others=()):
    parts, features, _ = got.shape
    count = rank.shape[1]

    def kernel(base_ref, rank_ref, got_ref, *refs):
        out_ref = refs[-1]
        place = base_ref[0] + lax.broadcasted_iota(i32, (slots, count), 0)
        total = jnp.zeros((features, count), f32)
        for part in range(parts):
            hit = rank_ref[parts + part : parts + part + 1, :] == place
            total += nn(got_ref[part], hit.astype(f32).astype(bf16))
        out_ref[0] = total[:, : count // 2].astype(bf16)
        out_ref[1] = total[:, count // 2 :].astype(bf16)

    return call(
        kernel,
        shape_of((2, features, count // 2), bf16),
        (rank, got, *others),
        scalars=(base.reshape(1),),
        in_specs=[None, None] + [pl.BlockSpec(memory_space=pl.ANY)] * len(others),
    )


def embed(tokens, table, me, before, beside):
    rank, most = ranks(tokens, me, table.shape[1])

    def more(state):
        base, held = state
        sent = pick(tokens, rank, table, me, base)
        got = lax.all_to_all(sent, "rep", 0, 0, tiled=True)
        return base + slots, held + place_slots(rank, got, base)

    base = jnp.zeros((), i32)
    sent = after(pick(tokens, rank, table, me, base), *before)
    got = lax.all_to_all(sent, "rep", 0, 0, tiled=True)
    beside = beside(before)
    first = place_slots(rank, got, base, beside)
    _, held = lax.while_loop(
        lambda state: state[0] < most[0], more, (jnp.full((), slots, i32), first)
    )
    return held, beside


def to_rows(core, kept, got):
    features, count = kept.shape

    def kernel(core_ref, kept_ref, got_ref, plain_ref, power_ref):
        low = core_ref[0] == 0
        kept, got = kept_ref[...].astype(f32), got_ref[...].astype(f32)
        both = jnp.concatenate([jnp.where(low, kept, got), jnp.where(low, got, kept)], axis=0)
        plain_ref[...] = both.T.astype(bf16)
        power = jnp.sum(both * both, axis=0, keepdims=True)
        for part in range(count // 128):
            power_ref[part : part + 1, :] = power[:, part * 128 : (part + 1) * 128]

    return call(
        kernel,
        (shape_of((count, 2 * features), bf16), shape_of((count // 128, 128), f32)),
        (kept, got),
        scalars=(core.reshape(1),),
    )


def across_chips(value):
    value = value + to_tp(value, 1, 0)
    for mask in (1, 3):
        route = [(place, place ^ (mask << 1)) for place in range(16)]
        value = value + lax.ppermute(value, "tp", route)
    return value


def reduce_own(core, chip, plain, power, gain, slices_own, slices_other, tenants):
    count, features = plain.shape
    width = gain.size
    parts, tenant_count, rank_part, packed_width = slices_own.shape
    skip = packed_width - features // 2

    def kernel(
        core_ref, chip_ref, plain_ref, power_ref, gain_ref, own_ref, other_ref, tenant_ref,
        scale_ref, out_ref,
    ):
        low = core_ref[0] == 0
        scale = lax.rsqrt(power_ref[...] / width + epsilon)
        scale = jnp.concatenate(
            [
                jnp.broadcast_to(scale[part : part + 1, :], (128, 128)).T
                for part in range(count // 128)
            ],
            axis=0,
        )
        scale_ref[...] = scale
        normed = (plain_ref[...].astype(f32) * scale[:, :1] * gain_ref[0]).astype(bf16)
        reduced = jnp.zeros((count, parts * rank_part), f32)
        for tenant in range(tenant_count):
            own = jnp.concatenate([own_ref[part, tenant, :, skip:] for part in range(parts)], axis=0)
            other = jnp.concatenate(
                [other_ref[part, tenant, :, skip:] for part in range(parts)], axis=0
            )
            own, other = own.astype(f32), other.astype(f32)
            down = jnp.concatenate(
                [jnp.where(low, own, other), jnp.where(low, other, own)], axis=1
            ).astype(bf16)
            reduced += jnp.where(tenant_ref[...] == tenant, nt(normed, down), 0.0)
        out_ref[...] = reduced

    return call(
        kernel,
        (shape_of((count, 128), f32), shape_of((count, parts * rank_part), f32)),
        (plain, power, gain, slices_own, slices_other, tenants),
        scalars=(core.reshape(1), chip.reshape(1)),
        in_specs=[
            None,
            None,
            pl.BlockSpec((1, 1, features), lambda step, core, chip: (chip[0], 0, 0)),
            None,
            None,
            None,
        ],
        flops=2 * features * count * parts * tenant_count * rank_part,
        room=12,
    )


def next_gather(left, right, across):
    half = left.shape[0] // 2

    def kernel(left_ref, right_ref, across_ref, up_ref, down_ref, over_ref):
        up_ref[:half] = left_ref[:half]
        up_ref[half:] = across_ref[:half]
        down_ref[:half] = right_ref[half:]
        down_ref[half:] = across_ref[half:]
        over_ref[:half] = left_ref[half:]
        over_ref[half:] = right_ref[:half]

    sent = shape_of(left.shape, bf16)
    return call(kernel, (sent, sent, sent), (left, right, across))


def last_gather(up, down, cut):
    count, features = up.shape
    half = count // 2
    first, second = cut

    def kernel(up_ref, down_ref, right_ref, left_ref, across_ref):
        right_ref[...] = up_ref[half : half + first]
        left_ref[...] = down_ref[second:]
        across_ref[: half - first] = up_ref[first:half]
        across_ref[half - first :] = down_ref[: second - half]

    return call(
        kernel,
        tuple(
            shape_of((rows, features), bf16) for rows in (first, count - second, second - first)
        ),
        (up, down),
    )


def project(places, pieces, scale, gain, weights, total=None, finish=None):
    arrays = []
    layout = []
    for piece in pieces:
        entry = []
        for array, start, rows in piece:
            known = [index for index, held in enumerate(arrays) if held is array]
            if not known:
                arrays.append(array)
                known = [len(arrays) - 1]
            entry.append((known[0], start, rows))
        layout.append(entry)
    count = sum(rows for _, _, rows in pieces[0])
    query_own, query_other, pairs = weights
    columns = query_own.shape[1]
    chip_width = query_own.shape[0] // 8
    has_total = total is not None
    steps = 2
    part = columns // steps
    many = len(pieces)

    def kernel(places_ref, *refs):
        del places_ref
        refs = list(refs)
        taken = [refs.pop(0) for _ in arrays]
        scale_ref = refs.pop(0)
        gain_refs = [refs.pop(0) for _ in pieces]
        own_refs = [refs.pop(0) for _ in pieces]
        other_refs = [refs.pop(0) for _ in pieces]
        pair_refs = [refs.pop(0) for _ in pieces]
        total_refs = [refs.pop(0) for _ in range(3)] if has_total else None
        finish_refs = [refs.pop(0) for _ in range(9)] if finish is not None else None
        outs, sums = (refs[:-3], refs[-3:]) if finish is not None else ([], refs)
        step = pl.program_id(0)
        rows = []
        for entry, gain_ref in zip(layout, gain_refs):
            plain = [taken[at][first : first + size] for at, first, size in entry]
            plain = jnp.concatenate(plain, axis=0).astype(f32)
            rows.append((plain * scale_ref[:, :1] * gain_ref[0]).astype(bf16))
        rows = jnp.concatenate(rows, axis=1)
        for side, weight_refs in enumerate((own_refs, other_refs)):
            result = nn(rows, jnp.concatenate([ref[...] for ref in weight_refs], axis=0))
            if has_total:
                result += total_refs[side][...]
            if finish is None:
                sums[side][...] = result
            else:
                sums[side][:, pl.ds(pl.multiple_of(step * part, part), part)] = result

        @pl.when(step == 0)
        def _():
            result = nt(rows, jnp.concatenate([ref[...] for ref in pair_refs], axis=1))
            if has_total:
                result += total_refs[2][...]
            sums[2][...] = result

        if finish is not None:

            @pl.when(step == steps - 1)
            def _():
                finish_kernel(finish_refs, sums, outs)

    def weight_spec(index):
        return pl.BlockSpec((chip_width, part), lambda step, places: (places[index], step))

    def pair_spec(index):
        return pl.BlockSpec((pairs.shape[0], chip_width), lambda step, places: (0, places[index]))

    sum_spec = pl.BlockSpec((count, part), lambda step, places: (0, step))
    sums = (
        shape_of((count, columns), f32),
        shape_of((count, columns), f32),
        shape_of((count, pairs.shape[0]), f32),
    )
    sum_specs = (sum_spec, sum_spec, whole(sums[2]))
    def gain_spec(index):
        return pl.BlockSpec((1, 1, chip_width), lambda step, places: (places[index], 0, 0))

    in_specs = [None] * (len(arrays) + 1)
    in_specs += [gain_spec(index) for index in range(many)]
    in_specs += [weight_spec(index) for index in range(many)] * 2
    in_specs += [pair_spec(index) for index in range(many)]
    operands = arrays + [scale] + [gain] * many + [query_own] * many + [query_other] * many + [pairs] * many
    if has_total:
        operands += list(total)
        in_specs += list(sum_specs)
    if finish is None:
        out_shape, out_specs, scratch = sums, sum_specs, []
    else:
        operands += list(finish)
        in_specs += [None] * 9
        out_shape = (
            shape_of((count, 2 * columns), f32),
            shape_of((count, pairs.shape[0] // 2), bf16),
            shape_of((count, pairs.shape[0] // 2), bf16),
        )
        out_specs = None
        scratch = [pltpu.VMEM(sum_.shape, f32) for sum_ in sums]
    return call(
        kernel,
        out_shape,
        operands,
        scalars=(places,),
        grid=(steps,),
        in_specs=in_specs,
        out_specs=out_specs,
        scratch=scratch,
        flops=2 * many * count * chip_width * (2 * columns + pairs.shape[0]),
        room=28,
    )


def finish_kernel(refs, sums, outs):
    core_ref, reduced_ref, tenant_ref, own_ref, other_ref, query_gain_ref, key_gain_ref = refs[:7]
    cosine, sine = refs[7][...], refs[8][...]
    out_query_ref, out_key_ref, out_value_ref = outs
    parts, tenant_count = own_ref.shape[:2]
    columns = sums[0].shape[1]
    low_rank = reduced_ref[...].astype(bf16).astype(f32)
    head_size = cosine.shape[1]

    def head_norm(vector, gain):
        power = jnp.mean(vector * vector, axis=-1, keepdims=True)
        vector = vector * lax.rsqrt(power + epsilon) * gain
        return vector * cosine + pltpu.roll(vector, head_size // 2, 1) * sine

    spread = jnp.concatenate(
        [
            jnp.where(tenant_ref[...] == tenant, low_rank, 0.0).astype(bf16)
            for tenant in range(tenant_count)
        ],
        axis=1,
    )
    for side, up_ref in enumerate((own_ref, other_ref)):
        up = jnp.concatenate(
            [
                up_ref[part, tenant, :, :columns]
                for tenant in range(tenant_count)
                for part in range(parts)
            ],
            axis=0,
        )
        delta = nn(spread, up)
        for head in range(columns // head_size):
            near = slice(head * head_size, (head + 1) * head_size)
            query = sums[side][:, near] + adapter_scale * delta[:, near]
            query = head_norm(query, query_gain_ref[...])
            spot = slice(side * columns + near.start, side * columns + near.stop)
            out_query_ref[:, spot] = query.astype(bf16).astype(f32)
    low = core_ref[0, 0] == 0
    both = sums[2][...]
    key = both[:, :head_size].astype(bf16).astype(f32)
    value = both[:, head_size:]
    key = jnp.where(low, key, pltpu.roll(key, head_size // 2, 1))
    value = jnp.where(low, value, pltpu.roll(value, head_size // 2, 1))
    out_key_ref[...] = head_norm(key, key_gain_ref[...]).astype(bf16)
    out_value_ref[...] = value.astype(bf16)


def allowed_below(block_size, step_count, group):
    table = np.full((2, 2, group * 2 * step_count, 4 * block_size + 4 * step_count), 1 << 20, np.int32)
    for row in range(table.shape[2]):
        pair_row, step = row // step_count % 2, row % step_count
        for core in range(2):
            for side in range(2):
                start = side * 2 * block_size + pair_row * block_size
                first = (core if side == 0 else 1 - core) * block_size
                table[core, :, row, start : start + block_size] = first + np.arange(block_size)
            for pair in range(2):
                start = 4 * block_size + (2 * pair + pair_row) * step_count
                table[core, pair, row, start : start + step + 1] = -1
    return table


def attend(core, lengths, query, new_keys, new_values, caches, step_count):
    count, query_width = query.shape
    block_size, head_size = caches[0].shape[1:]
    group = query_width // head_size
    rows_a_step = 8
    block = rows_a_step * step_count
    half_rows = count // step_count
    grid = half_rows // rows_a_step
    score_scale = head_size ** (-0.5)
    limits = allowed_below(block_size, step_count, group)

    def kernel(
        core_ref, lengths_ref, query_ref, new_key_ref, new_value_ref, own_key_ref, other_key_ref,
        own_value_ref, other_value_ref, limit_ref, out_ref,
    ):
        first = core_ref[0] * half_rows + pl.program_id(0) * rows_a_step
        pair_tokens = 2 * step_count
        pairs = range(rows_a_step // 2)
        row = lax.broadcasted_iota(i32, (group * pair_tokens, 1), 0) // step_count % 2
        fresh = [slice(pair // 2 * 4 * step_count, (pair // 2 + 1) * 4 * step_count) for pair in pairs]

        def joined(pair, own, other, new):
            near = 2 * pair
            return jnp.concatenate(
                [own[near], own[near + 1], other[near], other[near + 1], new[fresh[pair], :]], axis=0
            )

        scores = []
        for pair in pairs:
            tokens = slice(pair * pair_tokens, (pair + 1) * pair_tokens)
            queries = [
                query_ref[tokens, head * head_size : (head + 1) * head_size] for head in range(group)
            ]
            queries = jnp.concatenate(queries, axis=0).astype(bf16)
            scores.append(nt(queries, joined(pair, own_key_ref, other_key_ref, new_key_ref)))
        weights, totals = [], []
        for pair in pairs:
            length = jnp.where(
                row == 0, lengths_ref[first + 2 * pair], lengths_ref[first + 2 * pair + 1]
            )
            seen = limit_ref[0, pair % 2] < length
            masked = jnp.where(seen, scores[pair] * score_scale, masked_score)
            weight = jnp.exp(masked - jnp.max(masked, axis=1, keepdims=True))
            totals.append(jnp.sum(weight, axis=1, keepdims=True))
            weights.append(weight.astype(bf16))
        results = []
        for pair in pairs:
            values = joined(pair, own_value_ref, other_value_ref, new_value_ref)
            results.append(nn(weights[pair], values) / totals[pair])
        for pair in pairs[::2]:
            for head in range(group):
                part = slice(head * pair_tokens, (head + 1) * pair_tokens)
                both = jnp.concatenate([results[pair][part], results[pair + 1][part]], axis=0)
                out_ref[fresh[pair], head * head_size : (head + 1) * head_size] = both.astype(bf16)

    rows_spec = lambda width: pl.BlockSpec((block, width), lambda step, *_: (step, 0))
    cache_spec = pl.BlockSpec(
        (rows_a_step, block_size, head_size),
        lambda step, core_ref, lengths_ref: (core_ref[0] * grid + step, 0, 0),
    )
    limit_spec = pl.BlockSpec(
        (1, *limits.shape[1:]), lambda step, core_ref, lengths_ref: (core_ref[0], 0, 0, 0)
    )
    keys_own, keys_other, values_own, values_other = caches
    return call(
        kernel,
        shape_of((count, query_width), bf16),
        (query, new_keys, new_values, keys_own, keys_other, values_own, values_other, limits),
        scalars=(core.reshape(1), lengths),
        grid=(grid,),
        in_specs=[rows_spec(query_width), rows_spec(head_size), rows_spec(head_size)]
        + [cache_spec] * 4
        + [limit_spec],
        out_specs=rows_spec(query_width),
        room=16,
        flops=4 * count * query_width * 2 * 2 * block_size,
    )


def out_blocks(places, attended, own, other, cut=None):
    count, width = attended.shape
    steps = places.shape[0]
    depth = own.shape[0]
    chip_width = own.shape[1] // 8

    def kernel(places_ref, attended_ref, own_ref, other_ref, *out_refs):
        del places_ref
        weight = jnp.concatenate([own_ref[...], other_ref[...]], axis=0)
        product = nn(attended_ref[...], weight).astype(bf16)
        if cut is None:
            out_refs[0][0] = product
        else:
            for ref, start, stop in zip(out_refs, (0, *cut), (*cut, count)):
                ref[...] = product[start:stop]

    weight_spec = pl.BlockSpec((depth, chip_width), lambda step, places: (0, places[step]))
    if cut is None:
        out_shape = shape_of((steps, count, chip_width), bf16)
        out_specs = pl.BlockSpec((1, count, chip_width), lambda step, places: (step, 0, 0))
    else:
        sizes = (cut[0], cut[1] - cut[0], count - cut[1])
        out_shape = tuple(shape_of((size, chip_width), bf16) for size in sizes)
        out_specs = None
    return call(
        kernel,
        out_shape,
        (attended, own, other),
        scalars=(places,),
        grid=(steps,),
        in_specs=[None, weight_spec, weight_spec],
        out_specs=out_specs,
        flops=2 * steps * count * width * chip_width,
        room=16,
    )


def plus(value, piece):
    return (value.astype(f32) + piece.astype(f32)).astype(bf16)


def second_round(blocks, from_left, from_right, from_across, cut):
    _, count, features = blocks.shape
    half = count // 2
    first, second = cut

    def kernel(blocks_ref, left_ref, right_ref, across_ref, up_ref, down_ref, over_ref):
        far, across_left, across_right = blocks_ref.at[0], blocks_ref.at[1], blocks_ref.at[2]
        up_ref[:first] = plus(across_left[:first], left_ref[...])
        up_ref[first:half] = across_left[first:half]
        up_ref[half:] = far[:half]
        down_ref[: second - half] = plus(across_right[half:second], right_ref[half - first :])
        down_ref[second - half : half] = across_right[second:]
        down_ref[half : second] = far[half:second]
        down_ref[second:] = plus(far[second:], across_ref[...])
        over_ref[:half] = across_left[half:]
        over_ref[half : half + first] = across_right[:first]
        over_ref[half + first :] = plus(across_right[first:half], right_ref[: half - first])

    sent = shape_of((count, features), bf16)
    return call(kernel, (sent, sent, sent), (blocks, from_left, from_right, from_across))


def third_round(blocks, from_left, from_right, from_across):
    _, count, features = blocks.shape
    half = count // 2

    def kernel(blocks_ref, left_ref, right_ref, across_ref, up_ref, down_ref, over_ref):
        left, right, across = blocks_ref.at[0], blocks_ref.at[1], blocks_ref.at[2]
        over_ref[:half] = plus(across[:half], left_ref[:half])
        over_ref[half:] = plus(across[half:], right_ref[:half])
        up_ref[:half] = plus(left[:half], left_ref[half:])
        up_ref[half:] = plus(left[half:], across_ref[:half])
        down_ref[:half] = plus(right[:half], across_ref[half:])
        down_ref[half:] = plus(right[half:], right_ref[half:])

    sent = shape_of((count, features), bf16)
    return call(kernel, (sent, sent, sent), (blocks, from_left, from_right, from_across))


def add_residual(core, blocks, plain, arrived):
    count, features = plain.shape
    half = features // 2

    def kernel(core_ref, blocks_ref, plain_ref, up_ref, down_ref, over_ref, keep_ref, pass_ref):
        total = blocks_ref[0].astype(f32) + up_ref[...].astype(f32)
        total += down_ref[...].astype(f32) + over_ref[...].astype(f32)
        total = plain_ref[...].astype(f32) + total
        low = core_ref[0] == 0
        first, second = total[:, :half], total[:, half:]
        keep_ref[...] = jnp.where(low, first, second).astype(bf16)
        pass_ref[...] = jnp.where(low, second, first).astype(bf16)

    part = shape_of((count, half), bf16)
    own = pl.BlockSpec((1, count, features), lambda step, core_ref: (3, 0, 0))
    return call(
        kernel,
        (part, part),
        (blocks, plain, *arrived),
        scalars=(core.reshape(1),),
        in_specs=[own] + [None] * 4,
    )


def to_steps(core, kept, got, step_count):
    count, features = kept.shape
    half_rows = count // step_count
    row_count = 2 * half_rows

    def kernel(core_ref, kept_ref, got_ref, out_ref):
        low = core_ref[0] == 0
        kept, got = kept_ref[...].astype(f32), got_ref[...].astype(f32)
        both = jnp.concatenate([jnp.where(low, kept, got), jnp.where(low, got, kept)], axis=0)
        token = lax.broadcasted_iota(i32, (2 * count, 2 * count), 0)
        column = lax.broadcasted_iota(i32, (2 * count, 2 * count), 1)
        target = token % step_count * row_count + token // step_count
        order = (column == target).astype(f32).astype(bf16)
        turned = nn(both.T.astype(bf16), order)
        for step in range(step_count):
            out_ref[step] = turned[:, step * row_count : (step + 1) * row_count].astype(bf16)

    return call(
        kernel,
        shape_of((step_count, features, row_count), bf16),
        (kept, got),
        scalars=(core.reshape(1),),
    )


def on_device(
    step_token_index,
    row_tenant_index,
    stored_lengths,
    embedding,
    input_norm_gain,
    query_weight,
    key_weight,
    value_weight,
    output_weight,
    query_norm_gain,
    key_norm_gain,
    adapter_down_weight,
    adapter_up_weight,
    stored_keys,
    stored_values,
):
    replica_count = lax.axis_size("rep")
    step_count = step_token_index.shape[0]
    row_count = row_tenant_index.shape[0]
    half_rows = row_count // 2
    count = step_count * half_rows
    own_width = embedding.shape[1]
    chip_width = 2 * own_width
    head_size = query_norm_gain.shape[0]
    half_dim = head_size // 2
    tenant_count, _, rank_part = adapter_down_weight.shape
    me = lax.axis_index("rep")
    tp = lax.axis_index("tp")
    core = tp % 2
    chip = tp // 2

    packed = jnp.concatenate([adapter_up_weight, adapter_down_weight.transpose(0, 2, 1)], axis=2)
    key_own, value_own = key_weight.T, value_weight.T
    before = (
        over_replicas(packed),
        to_partner(query_weight),
        to_partner(key_own),
        to_partner(value_own),
    )

    def beside(before):
        slices, query_other, key_other, value_other = before
        mine = core * half_rows
        lengths = lax.dynamic_slice_in_dim(stored_lengths, mine, half_rows, 0)
        tenants = lax.dynamic_slice_in_dim(row_tenant_index, mine, half_rows, 0)
        tenants = jnp.repeat(tenants, step_count)[:, None]
        positions = (lengths[:, None] + jnp.arange(step_count)).reshape(count)
        cosine, sine = rope_tables(positions, half_dim)
        return (
            slices,
            to_partner(slices),
            query_other,
            jnp.concatenate([key_own, key_other, value_own, value_other]),
            to_partner(stored_keys),
            to_partner(stored_values),
            to_partner(output_weight),
            tenants,
            jnp.concatenate([cosine, cosine], axis=1),
            jnp.concatenate([-sine, sine], axis=1),
            input_norm_gain.reshape(8, 1, chip_width),
        )

    tokens = step_token_index.reshape(step_count, replica_count, 2, half_rows)
    tokens = tokens.transpose(1, 2, 3, 0).reshape(replica_count, 2 * count)
    held, beside = embed(tokens, embedding.T, me, before, beside)
    slices, slices_other, query_other, pairs, keys_other, values_other, output_other = beside[:7]
    tenants, cosine, sine, gain = beside[7:]
    kept = lax.dynamic_index_in_dim(held, core, 0, keepdims=False)
    passed = lax.dynamic_index_in_dim(held, 1 - core, 0, keepdims=False)
    own, power = to_rows(core, kept, to_partner(passed))

    z, y = chip // 4, chip % 4

    def places(*far):
        return jnp.stack([(z + dz) % 2 * 4 + (y + dy) % 4 for dz, dy in far])

    half = count // 2
    third = count // 3 // 16 * 16
    cut = (third, 2 * third)
    left, right, across = to_tp(own, 0, 1), to_tp(own, 0, -1), to_tp(own, 1, 0)
    power = across_chips(power)
    scale, reduced = reduce_own(core, chip, own, power, gain, slices, slices_other, tenants)
    reduced = across_chips(reduced)
    up, down, over = next_gather(left, right, across)
    up, down, over = to_tp(up, 0, 1), to_tp(down, 0, -1), to_tp(over, 1, 0)
    weights = (query_weight, query_other, pairs)
    total = project(
        places((0, 0), (0, -1), (0, 1), (1, 0)),
        [[(own, 0, count)], [(left, 0, count)], [(right, 0, count)], [(across, 0, count)]],
        scale,
        gain,
        weights,
    )
    last_up, last_down, last_over = last_gather(up, down, cut)
    last_up, last_down = to_tp(last_up, 0, 1), to_tp(last_down, 0, -1)
    last_over = to_tp(last_over, 1, 0)
    total = project(
        places((0, 2), (1, -1), (1, 1)),
        [
            [(up, 0, half), (down, 0, half)],
            [(up, half, half), (over, 0, half)],
            [(over, half, half), (down, half, half)],
        ],
        scale,
        gain,
        weights,
        total,
    )
    query, new_keys, new_values = project(
        places((1, 2)),
        [[(last_up, 0, third), (last_over, 0, third), (last_down, 0, count - 2 * third)]],
        scale,
        gain,
        weights,
        total,
        (
            core.reshape(1, 1),
            reduced,
            tenants,
            slices,
            slices_other,
            query_norm_gain[None],
            key_norm_gain[None],
            cosine,
            sine,
        ),
    )

    attended = attend(
        core,
        stored_lengths,
        query,
        new_keys,
        new_values,
        (stored_keys, keys_other, stored_values, values_other),
        step_count,
    )

    out_weights = attended, output_weight, output_other
    sent = out_blocks(places((1, 2)), *out_weights, cut)
    arrived = to_tp(sent[0], 0, 1), to_tp(sent[1], 0, -1), to_tp(sent[2], 1, 0)
    blocks = out_blocks(places((0, 2), (1, 1), (1, -1)), *out_weights)
    sent = second_round(blocks, *arrived, cut)
    arrived = to_tp(sent[0], 0, 1), to_tp(sent[1], 0, -1), to_tp(sent[2], 1, 0)
    blocks = out_blocks(places((0, 1), (0, -1), (1, 0), (0, 0)), *out_weights)
    sent = third_round(blocks, *arrived)
    arrived = to_tp(sent[0], 0, 1), to_tp(sent[1], 0, -1), to_tp(sent[2], 1, 0)
    kept, passed = add_residual(core, blocks, own, arrived)
    result = to_steps(core, kept, to_partner(passed), step_count)
    return result.transpose(0, 2, 1)


def solution(mesh):
    return jax.shard_map(
        on_device,
        mesh=mesh,
        in_specs=(
            P(),
            P("rep"),
            P("rep"),
            P("rep", "tp"),
            P(),
            P(None, "tp"),
            P(None, "tp"),
            P(None, "tp"),
            P("tp", None),
            P(),
            P(),
            P(None, "tp", "rep"),
            P(None, "rep", "tp"),
            P("rep", "tp", None),
            P("rep", "tp", None),
        ),
        out_specs=P(None, "rep", "tp"),
        check_vma=False,
    )
```

time: 663 us -> 169 us (0.25); the launches traced: 651 us -> 168 us
  local copies, waits for them, and re-layouts: 309 us -> 17 us
  waiting for transfers between devices: 195 us -> 30.9 us
  Pallas kernels: 0 us -> 51 us
  starting transfers between devices: 12.4 us -> 60.5 us
  blocking collectives: 47.6 us -> 0 us
  matrix products: 40.5 us -> 0 us
  other arithmetic: 32.8 us -> 7.14 us
  between operations: 13.9 us -> 0.63 us
    unnamed x44 -> x70, local copies, waits for them, and re-layouts: 279 us -> 12.2 us
    unnamed x6 -> x0, waiting for transfers between devices: 152 us -> none
    pallas_call x0 -> x19, Pallas kernels: none -> 51 us  [the longest x18 51 us: call(): pl.pallas_call(kernel, out_shape=out_shape, grid_spec=pltpu.PrefetchScala...]
    all_gather x2 -> x0, blocking collectives: 47.6 us -> none  [the longest x1 24.9 us: on_device(): lax.all_gather(adapter_up_weight, 'rep', axis=1, tiled=True)]
    all_gather x2 -> x0, waiting for transfers between devices: 43.3 us -> none  [the longest x1 36.7 us: on_device(): down_full = lax.all_gather(down_local, 'tp', axis=1, tiled=True)]
    dot_general x13 -> x0, matrix products: 40.5 us -> none  [the longest x1 7.1 us: on_device(): jnp.einsum('nd,edr->ner', normed_rows, down_full, preferred_element_type=...]
    ppermute x4 -> x33, starting transfers between devices: 12.3 us -> 50.8 us  [the longest x20 30.6 us: to_tp(): return lax.ppermute(block, 'tp', tp_route(dz, dy, 0))]
    gather x2 -> x0, local copies, waits for them, and re-layouts: 25.7 us -> none  [on_device(): picked = jnp.take(embedding, jnp.clip(local_ids, 0, vocab_rows - 1), axis=0)]
  transfers between devices with their start and end apart: 8 -> 35, of which waited for: 4 -> 11; matrix products, arithmetic and copies ran while one was open for 10% -> 7% of each run, Pallas kernels for 0% -> 19%
where the time goes in v1:
time: 169 us; the launch traced here: 168 us
  starting transfers between devices  60.5 us (36%)
  Pallas kernels  51 us (30%)
  waiting for transfers between devices  30.9 us (18%)
  local copies, waits for them, and re-layouts  17 us (10%)
  other arithmetic  7.14 us (4%)
    pallas_call x18, Pallas kernels, call(): pl.pallas_call(kernel, out_shape=out_shape, grid_spec=pltpu.PrefetchScala...  51 us
    ppermute x20, starting transfers between devices, to_tp(): return lax.ppermute(block, 'tp', tp_route(dz, dy, 0))  30.6 us
    ppermute x9, starting transfers between devices, to_partner(): return lax.ppermute(block, 'tp', tp_route(0, 0, 1))  14.8 us
    unnamed x70, local copies, waits for them, and re-layouts  12.2 us
    ppermute x20, waiting for transfers between devices, to_tp(): return lax.ppermute(block, 'tp', tp_route(dz, dy, 0))  11.1 us
    all_to_all x1, waiting for transfers between devices, embed(): got = lax.all_to_all(sent, 'rep', 0, 0, tiled=True)  9.81 us
    ppermute x4, waiting for transfers between devices, across_chips(): value = value + lax.ppermute(value, 'tp', route)  6.73 us
    all_to_all x1, starting transfers between devices, over_replicas(): return lax.all_to_all(copies, 'rep', 0, 0, tiled=True)  5.46 us
  transfers between devices with their start and end apart: 35, of which 11 were waited for; matrix products, arithmetic and copies ran while one was open for 7% of the time, Pallas kernels for 19%

profile of v1, /device:TPU:1, one launch (start us, length us, event | category | flops | bytes accessed | tf_op | source)
XLA Modules:
  0.0 167.8 jit_solution(163129972192912168)
XLA Ops:
  5.1 5.5 %all-to-all-start.1 = ((bf16[8,4,16,832]{3,2,1,0:T(8,128)(2,1)}), bf16[8,4,16,832]{3,2,1,0:T(8,128)(2,1)}, u32[]{:S(2)}, u32[]{:S(2)}) async-start(bf16[8,4,16,832]{3,2,1,0:T(8,128)(2,1)} %broadcast_in_dim.8), calls=%async_computation.1 | async-start | bytes 1835008 | tf_op jit(solution)/shard_map/all_to_all | solution.py:39
  12.9 10.2 %shard_map.155.refs_0_ = bf16[8,320,128]{2,1,0:T(8,128)(2,1)S(1)} custom-call(s32[1]{0:T(128)} %bitcast.9.me_ref, s32[1]{0:T(128)} %constant.146.clone.1.base_ref, s32[8,512]{1,0:T(8,128)S(1)} %copy.20.tokens_ref, s32[16,512]{1,0:T(8,128)S(1)} %get-tuple-element.185.rank_ref, bf16[320,9496]{1,0:T(8,128)(2,1)} %bitcast.57), custom_call_target="tpu_custom_call" | custom-call | flops 6223298560 | bytes 6126592 | tf_op jit(solution)/shard_map/pallas_call | solution.py:80
  28.2 4.2 %all-to-all-start.2 = ((bf16[8,320,128]{2,1,0:T(8,128)(2,1)}), bf16[8,320,128]{2,1,0:T(8,128)(2,1)}, u32[]{:S(2)}, u32[]{:S(2)}) async-start(bf16[8,320,128]{2,1,0:T(8,128)(2,1)} %shard_map.156), calls=%async_computation.2 | async-start | bytes 1310720 | tf_op jit(solution)/shard_map/all_to_all | solution.py:243
  34.3 9.8 %all-to-all-done.2.got_ref = bf16[8,320,128]{2,1,0:T(8,128)(2,1)} async-done(((bf16[8,320,128]{2,1,0:T(8,128)(2,1)}), bf16[8,320,128]{2,1,0:T(8,128)(2,1)}, u32[]{:S(2)}, u32[]{:S(2)}) %all-to-all-start.2) | async-done | bytes 655392 | tf_op jit(solution)/shard_map/all_to_all | solution.py:243
  47.6 2.7 %shard_map.157 = bf16[2,320,256]{2,1,0:T(8,128)(2,1)} custom-call(s32[1]{0:T(128)} %constant.146.clone.1.base_ref, s32[16,512]{1,0:T(8,128)} %copy-done.29, bf16[8,320,128]{2,1,0:T(8,128)(2,1)} %all-to-all-done.2.got_ref, bf16[8,4,16,832]{3,2,1,0:T(8,128)(2,1)} %all-to-all-done.1.refs_1_.refs_0_.own_ref.refs_14_, ...), custom_call_target="tpu_custom_call" | custom-call | flops 1048576 | bytes 22074368 | tf_op jit(solution)/shard_map/pallas_call | solution.py:80
  54.0 3.4 %collective-permute-start.10 = (bf16[256,640]{1,0:T(8,128)(2,1)S(1)}, bf16[256,640]{1,0:T(8,128)(2,1)S(1)}, u32[]{:S(2)}, u32[]{:S(2)}) collective-permute-start(bf16[256,640]{1,0:T(8,128)(2,1)S(1)} %get-tuple-element.78.plain_ref.refs_0_), channel_id=1, source_target_pairs={{0,8},{1,9},{2,10},{3,11},{4,12},{5,13},{6,14},{7,15},{8,0},{9,1},... | collective-permute-start | bytes 983048 | tf_op jit(solution)/shard_map/ppermute | solution.py:29
  60.3 4.9 %collective-permute-done.16 = f32[2,128]{1,0:T(2,128)S(1)} collective-permute-done((f32[2,128]{1,0:T(2,128)S(1)}, f32[2,128]{1,0:T(2,128)S(1)}, u32[]{:S(2)}, u32[]{:S(2)}) %collective-permute-start.16) | collective-permute-done | bytes 1056 | tf_op jit(solution)/shard_map/ppermute | solution.py:29
  68.0 2.7 %collective-permute-start.18 = (f32[2,128]{1,0:T(2,128)S(1)}, f32[2,128]{1,0:T(2,128)S(1)}, u32[]{:S(2)}, u32[]{:S(2)}) collective-permute-start(f32[2,128]{1,0:T(2,128)S(1)} %add.192), channel_id=1, source_target_pairs={{0,6},{1,7},{2,4},{3,5},{4,2},{5,3},{6,0},{7,1},{8,14},{9,15},{10,... | collective-permute-start | bytes 3080 | tf_op jit(solution)/shard_map/ppermute | solution.py:276
  71.7 2.6 %shard_map.161 = (f32[256,128]{1,0:T(8,128)S(1)}, f32[256,128]{1,0:T(8,128)}) custom-call(s32[1]{0:T(128)} %bitcast.3.core_ref, s32[1]{0:T(128)} %bitcast.19.chip_ref, bf16[256,640]{1,0:T(8,128)(2,1)S(1)} %get-tuple-element.78.plain_ref.refs_0_, f32[2,128]{1,0:T(2,128)S(1)} %add.193.power_ref, f32[8,1,640]{2,1,0:T(1,128)S(1)} %bitcast.40, ...), custom_call_target="tpu_custom_call" | custom-call | flops 167772160 | bytes 2054144 | tf_op jit(solution)/shard_map/pallas_call | solution.py:80
  78.2 2.7 %collective-permute-start.12 = (bf16[256,640]{1,0:T(8,128)(2,1)}, bf16[256,640]{1,0:T(8,128)(2,1)S(1)}, u32[]{:S(2)}, u32[]{:S(2)}) collective-permute-start(bf16[256,640]{1,0:T(8,128)(2,1)} %get-tuple-element.80), channel_id=1, source_target_pairs={{0,6},{1,7},{2,0},{3,1},{4,2},{5,3},{6,4},{7,5},{8,14},{9,15},{10,... | collective-permute-start | bytes 983048 | tf_op jit(solution)/shard_map/ppermute | solution.py:29
  84.0 4.3 %collective-permute-done.21 = f32[256,128]{1,0:T(8,128)} collective-permute-done((f32[256,128]{1,0:T(8,128)}, f32[256,128]{1,0:T(8,128)}, u32[]{:S(2)}, u32[]{:S(2)}) %collective-permute-start.21) | collective-permute-done | bytes 131104 | tf_op jit(solution)/shard_map/ppermute | solution.py:276
  99.2 5.0 %shard_map.162 = (f32[256,512]{1,0:T(8,128)S(1)}, f32[256,512]{1,0:T(8,128)S(1)}, f32[256,256]{1,0:T(8,128)S(1)}) custom-call(s32[4]{0:T(128)S(1)} %pad_add_fusion.2.places_ref, bf16[256,640]{1,0:T(8,128)(2,1)S(1)} %get-tuple-element.78.plain_ref.refs_0_, bf16[256,640]{1,0:T(8,128)(2,1)S(1)} %copy-done.12, bf16[256,640]{1,0:T(8,128)(2,1)S(1)} %copy-done.14, ...), custom_call_target="tpu_custom_call" | custom-call | flops 1677721600 | bytes 53952512 | tf_op jit(solution)/shard_map/pallas_call | solution.py:80
  104.4 2.7 %collective-permute-start.14 = (bf16[80,640]{1,0:T(8,128)(2,1)S(1)}, bf16[80,640]{1,0:T(8,128)(2,1)S(1)}, u32[]{:S(2)}, u32[]{:S(2)}) collective-permute-start(bf16[80,640]{1,0:T(8,128)(2,1)S(1)} %get-tuple-element.82), channel_id=1, source_target_pairs={{0,8},{1,9},{2,10},{3,11},{4,12},{5,13},{6,14},{7,15},{8,0},{9,1},... | collective-permute-start | bytes 307208 | tf_op jit(solution)/shard_map/ppermute | solution.py:29
  107.2 4.4 %shard_map.163 = (f32[256,512]{1,0:T(8,128)S(1)}, f32[256,512]{1,0:T(8,128)S(1)}, f32[256,256]{1,0:T(8,128)S(1)}) custom-call(s32[3]{0:T(128)S(1)} %pad_add_fusion.1.places_ref, bf16[256,640]{1,0:T(8,128)(2,1)S(1)} %collective-permute-done.11.up_ref.refs_0_, bf16[256,640]{1,0:T(8,128)(2,1)S(1)} %collective-permute-done.12.down_ref.refs_1_, ...), custom_call_target="tpu_custom_call" | custom-call | flops 1258291200 | bytes 41807872 | tf_op jit(solution)/shard_map/pallas_call | solution.py:80
  111.7 4.2 %shard_map.164 = (f32[256,1024]{1,0:T(8,128)S(1)}, bf16[256,128]{1,0:T(8,128)(2,1)S(1)}, bf16[256,128]{1,0:T(8,128)(2,1)S(1)}) custom-call(s32[1]{0:T(128)} %bitcast.8.places_ref, bf16[80,640]{1,0:T(8,128)(2,1)S(1)} %collective-permute-done.13.refs_0_, bf16[80,640]{1,0:T(8,128)(2,1)S(1)} %collective-permute-done.14.refs_1_, ...), custom_call_target="tpu_custom_call" | custom-call | flops 419430400 | bytes 16996356 | tf_op jit(solution)/shard_map/pallas_call | solution.py:80
  116.0 7.7 %shard_map.165.attended_ref = bf16[256,1024]{1,0:T(8,128)(2,1)S(1)} custom-call(s32[1]{0:T(128)} %bitcast.3.core_ref, s32[128]{0:T(128)S(1)} %copy-done.25, f32[256,1024]{1,0:T(8,128)S(1)} %get-tuple-element.94.query_ref, bf16[256,128]{1,0:T(8,128)(2,1)S(1)} %get-tuple-element.95.new_key_ref, bf16[256,128]{1,0:T(8,128)(2,1)S(1)} %get-tuple-element.96.new_value_ref, ...), custom_call_target="tpu_custom_call" | custom-call | flops 402653184 | bytes 14172160 | tf_op jit(solution)/shard_map/pallas_call | solution.py:80
  126.1 2.6 %collective-permute-start.24 = (bf16[80,640]{1,0:T(8,128)(2,1)S(1)}, bf16[80,640]{1,0:T(8,128)(2,1)S(1)}, u32[]{:S(2)}, u32[]{:S(2)}) collective-permute-start(bf16[80,640]{1,0:T(8,128)(2,1)S(1)} %get-tuple-element.98), channel_id=1, source_target_pairs={{0,6},{1,7},{2,0},{3,1},{4,2},{5,3},{6,4},{7,5},{8,14},{9,15},{10,... | collective-permute-start | bytes 307208 | tf_op jit(solution)/shard_map/ppermute | solution.py:29
  128.8 4.1 %shard_map.167.blocks_ref = bf16[3,256,640]{2,1,0:T(8,128)(2,1)S(1)} custom-call(s32[3]{0:T(128)S(1)} %pad_add_fusion.3.places_ref, bf16[256,1024]{1,0:T(8,128)(2,1)S(1)} %shard_map.165.attended_ref, bf16[512,5120]{1,0:T(8,128)(2,1)S(1)} %bitcast.38, bf16[512,5120]{1,0:T(8,128)(2,1)} %collective-permute-done.6.refs_6_.other_ref), custom_call_target="tpu_custom_call" | custom-call | flops 1006632960 | bytes 11010048 | tf_op jit(solution)/shard_map/pallas_call | solution.py:80
  133.1 2.7 %collective-permute-start.27 = (bf16[256,640]{1,0:T(8,128)(2,1)S(1)}, bf16[256,640]{1,0:T(8,128)(2,1)S(1)}, u32[]{:S(2)}, u32[]{:S(2)}) collective-permute-start(bf16[256,640]{1,0:T(8,128)(2,1)S(1)} %get-tuple-element.101), channel_id=1, source_target_pairs={{0,6},{1,7},{2,0},{3,1},{4,2},{5,3},{6,4},{7,5},{8,14},{9,15},{10,... | collective-permute-start | bytes 983048 | tf_op jit(solution)/shard_map/ppermute | solution.py:29
  138.3 4.8 %shard_map.166.blocks_ref = bf16[4,256,640]{2,1,0:T(8,128)(2,1)S(1)} custom-call(s32[4]{0:T(128)S(1)} %pad_add_fusion.places_ref, bf16[256,1024]{1,0:T(8,128)(2,1)S(1)} %shard_map.165.attended_ref, bf16[512,5120]{1,0:T(8,128)(2,1)S(1)} %bitcast.38, bf16[512,5120]{1,0:T(8,128)(2,1)} %collective-permute-done.6.refs_6_.other_ref), custom_call_target="tpu_custom_call" | custom-call | flops 1342177280 | bytes 11010048 | tf_op jit(solution)/shard_map/pallas_call | solution.py:80
  143.5 2.7 %collective-permute-start.30 = (bf16[256,640]{1,0:T(8,128)(2,1)S(1)}, bf16[256,640]{1,0:T(8,128)(2,1)S(1)}, u32[]{:S(2)}, u32[]{:S(2)}) collective-permute-start(bf16[256,640]{1,0:T(8,128)(2,1)S(1)} %get-tuple-element.104), channel_id=1, source_target_pairs={{0,6},{1,7},{2,0},{3,1},{4,2},{5,3},{6,4},{7,5},{8,14},{9,15},{10,... | collective-permute-start | bytes 983048 | tf_op jit(solution)/shard_map/ppermute | solution.py:29
  148.6 2.9 %collective-permute-done.29.up_ref = bf16[256,640]{1,0:T(8,128)(2,1)S(1)} collective-permute-done((bf16[256,640]{1,0:T(8,128)(2,1)S(1)}, bf16[256,640]{1,0:T(8,128)(2,1)S(1)}, u32[]{:S(2)}, u32[]{:S(2)}) %collective-permute-start.29) | collective-permute-done | bytes 327712 | tf_op jit(solution)/shard_map/ppermute | solution.py:29
  151.5 3.2 %collective-permute-done.31.over_ref = bf16[256,640]{1,0:T(8,128)(2,1)S(1)} collective-permute-done((bf16[256,640]{1,0:T(8,128)(2,1)S(1)}, bf16[256,640]{1,0:T(8,128)(2,1)S(1)}, u32[]{:S(2)}, u32[]{:S(2)}) %collective-permute-start.31) | collective-permute-done | bytes 327712 | tf_op jit(solution)/shard_map/ppermute | solution.py:29
  155.1 10.5 %collective-permute-start.32 = (bf16[256,320]{1,0:T(8,128)(2,1)S(1)}, bf16[256,320]{1,0:T(8,128)(2,1)S(1)}, u32[]{:S(2)}, u32[]{:S(2)}) collective-permute-start(bf16[256,320]{1,0:T(8,128)(2,1)S(1)} %get-tuple-element.107), channel_id=1, source_target_pairs={{0,1},{1,0},{2,3},{3,2},{4,5},{5,4},{6,7},{7,6},{8,9},{9,8},{10,11... | collective-permute-start | bytes 491528 | tf_op jit(solution)/shard_map/ppermute | solution.py:33
  (164 shorter events, 57.1 us)
Async XLA Ops:
  0.0 28.2 %collective-permute-start = (bf16[5120,512]{1,0:T(8,128)(2,1)}, bf16[5120,512]{1,0:T(8,128)(2,1)}, u32[]{:S(2)}, u32[]{:S(2)}) collective-permute-start(bf16[5120,512]{1,0:T(8,128)(2,1)} %refs_5_.1), channel_id=1, source_target_pairs={{0,1},{1,0},{2,3},{3,2},{4,5},{5,4},{6,7},{7,6},{8,9},{9,8},{10,11... | collective-permute-start | bytes 15728648 | tf_op jit(solution)/shard_map/ppermute | solution.py:33
  1.4 32.9 %collective-permute-start.6 = (bf16[512,5120]{1,0:T(8,128)(2,1)}, bf16[512,5120]{1,0:T(8,128)(2,1)}, u32[]{:S(2)}, u32[]{:S(2)}) collective-permute-start(bf16[512,5120]{1,0:T(8,128)(2,1)} %own_ref.5), channel_id=1, source_target_pairs={{0,1},{1,0},{2,3},{3,2},{4,5},{5,4},{6,7},{7,6},{8,9},{9,8},{10,11... | collective-permute-start | bytes 15728648 | tf_op jit(solution)/shard_map/ppermute | solution.py:33
  1.4 32.9 %collective-permute-start.4 = (bf16[128,96,128]{2,1,0:T(8,128)(2,1)}, bf16[128,96,128]{2,1,0:T(8,128)(2,1)}, u32[]{:S(2)}, u32[]{:S(2)}) collective-permute-start(bf16[128,96,128]{2,1,0:T(8,128)(2,1)} %own_key_ref.1), channel_id=1, source_target_pairs={{0,1},{1,0},{2,3},{3,2},{4,5},{5,4},{6,7},{7,6},{8,9},{9,8},{10,11... | collective-permute-start | bytes 9437192 | tf_op jit(solution)/shard_map/ppermute | solution.py:33
  1.9 32.4 %collective-permute-start.5 = (bf16[128,96,128]{2,1,0:T(8,128)(2,1)}, bf16[128,96,128]{2,1,0:T(8,128)(2,1)}, u32[]{:S(2)}, u32[]{:S(2)}) collective-permute-start(bf16[128,96,128]{2,1,0:T(8,128)(2,1)} %own_value_ref.1), channel_id=1, source_target_pairs={{0,1},{1,0},{2,3},{3,2},{4,5},{5,4},{6,7},{7,6},{8,9},{9,8},{10,11... | collective-permute-start | bytes 9437192 | tf_op jit(solution)/shard_map/ppermute | solution.py:33
  1.9 10.5 %collective-permute-start.1 = (bf16[64,5120]{1,0:T(8,128)(2,1)}, bf16[64,5120]{1,0:T(8,128)(2,1)S(1)}, u32[]{:S(2)}, u32[]{:S(2)}) collective-permute-start(bf16[64,5120]{1,0:T(8,128)(2,1)} %bitcast.52), channel_id=1, source_target_pairs={{0,1},{1,0},{2,3},{3,2},{4,5},{5,4},{6,7},{7,6},{8,9},{9,8},{10,11... | collective-permute-start | bytes 1966088 | tf_op jit(solution)/shard_map/ppermute | solution.py:33
  5.1 20.1 %all-to-all-start.1 = ((bf16[8,4,16,832]{3,2,1,0:T(8,128)(2,1)}), bf16[8,4,16,832]{3,2,1,0:T(8,128)(2,1)}, u32[]{:S(2)}, u32[]{:S(2)}) async-start(bf16[8,4,16,832]{3,2,1,0:T(8,128)(2,1)} %broadcast_in_dim.8), calls=%async_computation.1 | async-start | bytes 1835008 | tf_op jit(solution)/shard_map/all_to_all | solution.py:39
  12.5 11.5 %collective-permute-start.2 = (bf16[64,5120]{1,0:T(8,128)(2,1)}, bf16[64,5120]{1,0:T(8,128)(2,1)S(1)}, u32[]{:S(2)}, u32[]{:S(2)}) collective-permute-start(bf16[64,5120]{1,0:T(8,128)(2,1)} %bitcast.54), channel_id=1, source_target_pairs={{0,1},{1,0},{2,3},{3,2},{4,5},{5,4},{6,7},{7,6},{8,9},{9,8},{10,11... | collective-permute-start | bytes 1966088 | tf_op jit(solution)/shard_map/ppermute | solution.py:33
  25.1 9.2 %collective-permute-start.3 = (bf16[8,4,16,832]{3,2,1,0:T(8,128)(2,1)}, bf16[8,4,16,832]{3,2,1,0:T(8,128)(2,1)S(1)}, u32[]{:S(2)}, u32[]{:S(2)}) collective-permute-start(bf16[8,4,16,832]{3,2,1,0:T(8,128)(2,1)} %all-to-all-done.1.refs_1_.refs_0_.own_ref.refs_14_), channel_id=1, source_target_pairs={{0,1},{1,0},{2,3},{3,2},{4,5},{5,4},{6,7},{7,6},{8,9},{9,8},{10,11... | collective-permute-start | bytes 2555912 | tf_op jit(solution)/shard_map/ppermute | solution.py:33
  28.2 15.9 %all-to-all-start.2 = ((bf16[8,320,128]{2,1,0:T(8,128)(2,1)}), bf16[8,320,128]{2,1,0:T(8,128)(2,1)}, u32[]{:S(2)}, u32[]{:S(2)}) async-start(bf16[8,320,128]{2,1,0:T(8,128)(2,1)} %shard_map.156), calls=%async_computation.2 | async-start | bytes 1310720 | tf_op jit(solution)/shard_map/all_to_all | solution.py:243
  54.0 22.5 %collective-permute-start.10 = (bf16[256,640]{1,0:T(8,128)(2,1)S(1)}, bf16[256,640]{1,0:T(8,128)(2,1)S(1)}, u32[]{:S(2)}, u32[]{:S(2)}) collective-permute-start(bf16[256,640]{1,0:T(8,128)(2,1)S(1)} %get-tuple-element.78.plain_ref.refs_0_), channel_id=1, source_target_pairs={{0,8},{1,9},{2,10},{3,11},{4,12},{5,13},{6,14},{7,15},{8,0},{9,1},... | collective-permute-start | bytes 983048 | tf_op jit(solution)/shard_map/ppermute | solution.py:29
  57.4 19.2 %collective-permute-start.8 = (bf16[256,640]{1,0:T(8,128)(2,1)S(1)}, bf16[256,640]{1,0:T(8,128)(2,1)S(1)}, u32[]{:S(2)}, u32[]{:S(2)}) collective-permute-start(bf16[256,640]{1,0:T(8,128)(2,1)S(1)} %get-tuple-element.78.plain_ref.refs_0_), channel_id=1, source_target_pairs={{0,2},{1,3},{2,4},{3,5},{4,6},{5,7},{6,0},{7,1},{8,10},{9,11},{10,... | collective-permute-start | bytes 983048 | tf_op jit(solution)/shard_map/ppermute | solution.py:29
  58.7 17.9 %collective-permute-start.9 = (bf16[256,640]{1,0:T(8,128)(2,1)S(1)}, bf16[256,640]{1,0:T(8,128)(2,1)S(1)}, u32[]{:S(2)}, u32[]{:S(2)}) collective-permute-start(bf16[256,640]{1,0:T(8,128)(2,1)S(1)} %get-tuple-element.78.plain_ref.refs_0_), channel_id=1, source_target_pairs={{0,6},{1,7},{2,0},{3,1},{4,2},{5,3},{6,4},{7,5},{8,14},{9,15},{10,... | collective-permute-start | bytes 983048 | tf_op jit(solution)/shard_map/ppermute | solution.py:29
  77.5 13.1 %collective-permute-start.11 = (bf16[256,640]{1,0:T(8,128)(2,1)}, bf16[256,640]{1,0:T(8,128)(2,1)S(1)}, u32[]{:S(2)}, u32[]{:S(2)}) collective-permute-start(bf16[256,640]{1,0:T(8,128)(2,1)} %get-tuple-element.79), channel_id=1, source_target_pairs={{0,2},{1,3},{2,4},{3,5},{4,6},{5,7},{6,0},{7,1},{8,10},{9,11},{10,... | collective-permute-start | bytes 983048 | tf_op jit(solution)/shard_map/ppermute | solution.py:29
  78.2 12.4 %collective-permute-start.12 = (bf16[256,640]{1,0:T(8,128)(2,1)}, bf16[256,640]{1,0:T(8,128)(2,1)S(1)}, u32[]{:S(2)}, u32[]{:S(2)}) collective-permute-start(bf16[256,640]{1,0:T(8,128)(2,1)} %get-tuple-element.80), channel_id=1, source_target_pairs={{0,6},{1,7},{2,0},{3,1},{4,2},{5,3},{6,4},{7,5},{8,14},{9,15},{10,... | collective-permute-start | bytes 983048 | tf_op jit(solution)/shard_map/ppermute | solution.py:29
  82.6 24.5 %collective-permute-start.19 = (bf16[256,640]{1,0:T(8,128)(2,1)}, bf16[256,640]{1,0:T(8,128)(2,1)}, u32[]{:S(2)}, u32[]{:S(2)}) collective-permute-start(bf16[256,640]{1,0:T(8,128)(2,1)} %copy-done.26), channel_id=1, source_target_pairs={{0,8},{1,9},{2,10},{3,11},{4,12},{5,13},{6,14},{7,15},{8,0},{9,1},... | collective-permute-start | bytes 983048 | tf_op jit(solution)/shard_map/ppermute | solution.py:29
  89.3 14.9 %collective-permute-start.22 = (f32[256,128]{1,0:T(8,128)S(1)}, f32[256,128]{1,0:T(8,128)S(1)}, u32[]{:S(2)}, u32[]{:S(2)}) collective-permute-start(f32[256,128]{1,0:T(8,128)S(1)} %add.198), channel_id=1, source_target_pairs={{0,6},{1,7},{2,4},{3,5},{4,2},{5,3},{6,0},{7,1},{8,14},{9,15},{10,... | collective-permute-start | bytes 393224 | tf_op jit(solution)/shard_map/ppermute | solution.py:276
  90.7 20.9 %collective-permute-start.15 = (bf16[96,640]{1,0:T(8,128)(2,1)S(1)}, bf16[96,640]{1,0:T(8,128)(2,1)S(1)}, u32[]{:S(2)}, u32[]{:S(2)}) collective-permute-start(bf16[96,640]{1,0:T(8,128)(2,1)S(1)} %get-tuple-element.83), channel_id=1, source_target_pairs={{0,6},{1,7},{2,0},{3,1},{4,2},{5,3},{6,4},{7,5},{8,14},{9,15},{10,... | collective-permute-start | bytes 368648 | tf_op jit(solution)/shard_map/ppermute | solution.py:29
  133.0 10.1 %collective-permute-start.26 = (bf16[256,640]{1,0:T(8,128)(2,1)S(1)}, bf16[256,640]{1,0:T(8,128)(2,1)S(1)}, u32[]{:S(2)}, u32[]{:S(2)}) collective-permute-start(bf16[256,640]{1,0:T(8,128)(2,1)S(1)} %get-tuple-element.100), channel_id=1, source_target_pairs={{0,2},{1,3},{2,4},{3,5},{4,6},{5,7},{6,0},{7,1},{8,10},{9,11},{10,... | collective-permute-start | bytes 983048 | tf_op jit(solution)/shard_map/ppermute | solution.py:29
  133.1 10.0 %collective-permute-start.27 = (bf16[256,640]{1,0:T(8,128)(2,1)S(1)}, bf16[256,640]{1,0:T(8,128)(2,1)S(1)}, u32[]{:S(2)}, u32[]{:S(2)}) collective-permute-start(bf16[256,640]{1,0:T(8,128)(2,1)S(1)} %get-tuple-element.101), channel_id=1, source_target_pairs={{0,6},{1,7},{2,0},{3,1},{4,2},{5,3},{6,4},{7,5},{8,14},{9,15},{10,... | collective-permute-start | bytes 983048 | tf_op jit(solution)/shard_map/ppermute | solution.py:29
  135.7 7.4 %collective-permute-start.28 = (bf16[256,640]{1,0:T(8,128)(2,1)S(1)}, bf16[256,640]{1,0:T(8,128)(2,1)S(1)}, u32[]{:S(2)}, u32[]{:S(2)}) collective-permute-start(bf16[256,640]{1,0:T(8,128)(2,1)S(1)} %get-tuple-element.102), channel_id=1, source_target_pairs={{0,8},{1,9},{2,10},{3,11},{4,12},{5,13},{6,14},{7,15},{8,0},{9,1},... | collective-permute-start | bytes 983048 | tf_op jit(solution)/shard_map/ppermute | solution.py:29
  143.4 8.1 %collective-permute-start.29 = (bf16[256,640]{1,0:T(8,128)(2,1)S(1)}, bf16[256,640]{1,0:T(8,128)(2,1)S(1)}, u32[]{:S(2)}, u32[]{:S(2)}) collective-permute-start(bf16[256,640]{1,0:T(8,128)(2,1)S(1)} %get-tuple-element.103), channel_id=1, source_target_pairs={{0,2},{1,3},{2,4},{3,5},{4,6},{5,7},{6,0},{7,1},{8,10},{9,11},{10,... | collective-permute-start | bytes 983048 | tf_op jit(solution)/shard_map/ppermute | solution.py:29
  143.5 8.0 %collective-permute-start.30 = (bf16[256,640]{1,0:T(8,128)(2,1)S(1)}, bf16[256,640]{1,0:T(8,128)(2,1)S(1)}, u32[]{:S(2)}, u32[]{:S(2)}) collective-permute-start(bf16[256,640]{1,0:T(8,128)(2,1)S(1)} %get-tuple-element.104), channel_id=1, source_target_pairs={{0,6},{1,7},{2,0},{3,1},{4,2},{5,3},{6,4},{7,5},{8,14},{9,15},{10,... | collective-permute-start | bytes 983048 | tf_op jit(solution)/shard_map/ppermute | solution.py:29
  146.1 8.6 %collective-permute-start.31 = (bf16[256,640]{1,0:T(8,128)(2,1)S(1)}, bf16[256,640]{1,0:T(8,128)(2,1)S(1)}, u32[]{:S(2)}, u32[]{:S(2)}) collective-permute-start(bf16[256,640]{1,0:T(8,128)(2,1)S(1)} %get-tuple-element.105), channel_id=1, source_target_pairs={{0,8},{1,9},{2,10},{3,11},{4,12},{5,13},{6,14},{7,15},{8,0},{9,1},... | collective-permute-start | bytes 983048 | tf_op jit(solution)/shard_map/ppermute | solution.py:29
  155.1 11.5 %collective-permute-start.32 = (bf16[256,320]{1,0:T(8,128)(2,1)S(1)}, bf16[256,320]{1,0:T(8,128)(2,1)S(1)}, u32[]{:S(2)}, u32[]{:S(2)}) collective-permute-start(bf16[256,320]{1,0:T(8,128)(2,1)S(1)} %get-tuple-element.107), channel_id=1, source_target_pairs={{0,1},{1,0},{2,3},{3,2},{4,5},{5,4},{6,7},{7,6},{8,9},{9,8},{10,11... | collective-permute-start | bytes 491528 | tf_op jit(solution)/shard_map/ppermute | solution.py:33
  (46 other events, 305.0 us)

commit v2 on v1

--- a/solution.py
+++ b/solution.py
@@ -37,12 +37,6 @@
     count = lax.axis_size("rep")
     copies = jnp.broadcast_to(block[None], (count, *block.shape))
     return lax.all_to_all(copies, "rep", 0, 0, tiled=True)
-
-
-def rope_tables(positions, half_dim):
-    inverse = rope_base ** (-jnp.arange(half_dim, dtype=jnp.float32) / half_dim)
-    angle = positions.astype(jnp.float32)[:, None] * inverse
-    return jnp.cos(angle), jnp.sin(angle)
 
 
 f32 = jnp.float32
@@ -104,6 +98,37 @@
         out_specs=anywhere,
         input_output_aliases={0: 0},
     )(value, *others)
+
+
+def row_tables(core, lengths, tenants, step_count, head_size, *others):
+    row_count = lengths.shape[0]
+    count = row_count // 2 * step_count
+    half_dim = head_size // 2
+    inverse = rope_base ** (-np.arange(half_dim, dtype=np.float32) / np.float32(half_dim))
+    inverse = np.concatenate([inverse, inverse]).astype(np.float32)[None]
+
+    def kernel(core_ref, lengths_ref, tenants_ref, inverse_ref, *refs):
+        out_ref = refs[-1]
+        token = lax.broadcasted_iota(i32, (count, row_count), 0)
+        row = lax.broadcasted_iota(i32, (count, row_count), 1)
+        chosen = row == core_ref[0] * (row_count // 2) + token // step_count
+        length = jnp.sum(jnp.where(chosen, lengths_ref[...], 0).astype(f32), axis=1, keepdims=True)
+        tenant = jnp.sum(jnp.where(chosen, tenants_ref[...], 0).astype(f32), axis=1, keepdims=True)
+        step = lax.broadcasted_iota(i32, (count, 1), 0) % step_count
+        angle = (length + step.astype(f32)) * inverse_ref[...]
+        lane = lax.broadcasted_iota(i32, (count, head_size), 1)
+        out_ref[:, :head_size] = jnp.cos(angle)
+        sine = jnp.sin(angle)
+        out_ref[:, head_size : 2 * head_size] = jnp.where(lane < half_dim, -sine, sine)
+        out_ref[:, 2 * head_size :] = jnp.broadcast_to(tenant, (count, head_size))
+
+    return call(
+        kernel,
+        shape_of((count, 3 * head_size), f32),
+        (lengths[None], tenants[None], inverse, *others),
+        scalars=(core.reshape(1),),
+        in_specs=[None] * 3 + [pl.BlockSpec(memory_space=pl.ANY)] * len(others),
+    )
 
 
 def ranks(tokens, me, vocab_rows):
@@ -202,51 +227,57 @@
         in_specs=[None, None, pl.BlockSpec((features, tile), lambda step, *_: (0, step))],
         scratch=[pltpu.VMEM((parts, slots), i32), pltpu.VMEM((features, parts * slots), f32)],
         flops=2 * features * vocab_rows * parts * slots,
-        room=20,
-    )
-
-
-def place_slots(rank, got, base, others=()):
+        room=12,
+    )
+
+
+def place_slots(core, rank, got, base, others=()):
     parts, features, _ = got.shape
     count = rank.shape[1]
-
-    def kernel(base_ref, rank_ref, got_ref, *refs):
-        out_ref = refs[-1]
+    half = count // 2
+
+    def kernel(core_ref, base_ref, rank_ref, got_ref, *refs):
+        kept_ref, passed_ref = refs[-2:]
         place = base_ref[0] + lax.broadcasted_iota(i32, (slots, count), 0)
         total = jnp.zeros((features, count), f32)
         for part in range(parts):
             hit = rank_ref[parts + part : parts + part + 1, :] == place
             total += nn(got_ref[part], hit.astype(f32).astype(bf16))
-        out_ref[0] = total[:, : count // 2].astype(bf16)
-        out_ref[1] = total[:, count // 2 :].astype(bf16)
-
-    return call(
-        kernel,
-        shape_of((2, features, count // 2), bf16),
+        low = core_ref[0] == 0
+        first, second = total[:, :half], total[:, half:]
+        kept_ref[...] = jnp.where(low, first, second).astype(bf16)
+        passed_ref[...] = jnp.where(low, second, first).astype(bf16)
+
+    columns = shape_of((features, half), bf16)
+    return call(
+        kernel,
+        (columns, columns),
         (rank, got, *others),
-        scalars=(base.reshape(1),),
+        scalars=(core.reshape(1), base.reshape(1)),
         in_specs=[None, None] + [pl.BlockSpec(memory_space=pl.ANY)] * len(others),
     )
 
 
-def embed(tokens, table, me, before, beside):
+def embed(tokens, table, me, core, before, beside):
     rank, most = ranks(tokens, me, table.shape[1])
 
     def more(state):
-        base, held = state
+        base, kept, passed = state
         sent = pick(tokens, rank, table, me, base)
         got = lax.all_to_all(sent, "rep", 0, 0, tiled=True)
-        return base + slots, held + place_slots(rank, got, base)
+        more_kept, more_passed = place_slots(core, rank, got, base)
+        return base + slots, kept + more_kept, passed + more_passed
 
     base = jnp.zeros((), i32)
-    sent = after(pick(tokens, rank, table, me, base), *before)
+    picked = pick(tokens, rank, table, me, base)
+    sent = after(picked, before)
     got = lax.all_to_all(sent, "rep", 0, 0, tiled=True)
-    beside = beside(before)
-    first = place_slots(rank, got, base, beside)
-    _, held = lax.while_loop(
-        lambda state: state[0] < most[0], more, (jnp.full((), slots, i32), first)
-    )
-    return held, beside
+    beside = beside(sent)
+    first = place_slots(core, rank, got, base, beside)
+    _, kept, passed = lax.while_loop(
+        lambda state: state[0] < most[0], more, (jnp.full((), slots, i32), *first)
+    )
+    return kept, passed, beside
 
 
 def to_rows(core, kept, got):
@@ -269,24 +300,44 @@
     )
 
 
-def across_chips(value):
-    value = value + to_tp(value, 1, 0)
-    for mask in (1, 3):
-        route = [(place, place ^ (mask << 1)) for place in range(16)]
-        value = value + lax.ppermute(value, "tp", route)
-    return value
-
-
-def reduce_own(core, chip, plain, power, gain, slices_own, slices_other, tenants):
+def stack_pairs(key, value, other, ready):
+    rows, columns = key.shape
+    tile = columns // 4
+
+    def kernel(key_ref, value_ref, other_ref, ready_ref, out_ref):
+        del ready_ref
+        out_ref[:rows] = key_ref[...]
+        out_ref[rows : 2 * rows] = other_ref[:rows]
+        out_ref[2 * rows : 3 * rows] = value_ref[...]
+        out_ref[3 * rows :] = other_ref[rows:]
+
+    tall = lambda many: pl.BlockSpec((many * rows, tile), lambda step: (0, step))
+    return call(
+        kernel,
+        shape_of((4 * rows, columns), bf16),
+        (key, value, other, ready),
+        grid=(4,),
+        in_specs=[tall(1), tall(1), tall(2), pl.BlockSpec(memory_space=pl.ANY)],
+        out_specs=tall(4),
+    )
+
+
+def to_other_side(value, mask):
+    route = [(place, place ^ (mask << 1)) for place in range(16)]
+    return lax.ppermute(value, "tp", route)
+
+
+def reduce_own(core, chip, plain, power, gain, slices, tables, *others):
     count, features = plain.shape
     width = gain.size
-    parts, tenant_count, rank_part, packed_width = slices_own.shape
+    parts, tenant_count, rank_part, packed_width = slices[0].shape
     skip = packed_width - features // 2
 
     def kernel(
-        core_ref, chip_ref, plain_ref, power_ref, gain_ref, own_ref, other_ref, tenant_ref,
-        scale_ref, out_ref,
+        core_ref, chip_ref, plain_ref, power_ref, gain_ref, own_ref, other_ref, tables_ref, *refs,
     ):
+        scale_ref, out_ref = refs[-2:]
+        tenant_rows = tables_ref[:, 2 * 128 :]
         low = core_ref[0] == 0
         scale = lax.rsqrt(power_ref[...] / width + epsilon)
         scale = jnp.concatenate(
@@ -300,48 +351,56 @@
         normed = (plain_ref[...].astype(f32) * scale[:, :1] * gain_ref[0]).astype(bf16)
         reduced = jnp.zeros((count, parts * rank_part), f32)
         for tenant in range(tenant_count):
-            own = jnp.concatenate([own_ref[part, tenant, :, skip:] for part in range(parts)], axis=0)
-            other = jnp.concatenate(
-                [other_ref[part, tenant, :, skip:] for part in range(parts)], axis=0
-            )
+            own, other = [
+                jnp.concatenate([ref[part, tenant, :, skip:] for part in range(parts)], axis=0)
+                for ref in (own_ref, other_ref)
+            ]
             own, other = own.astype(f32), other.astype(f32)
             down = jnp.concatenate(
                 [jnp.where(low, own, other), jnp.where(low, other, own)], axis=1
             ).astype(bf16)
-            reduced += jnp.where(tenant_ref[...] == tenant, nt(normed, down), 0.0)
+            reduced += jnp.where(tenant_rows == tenant, nt(normed, down), 0.0)
         out_ref[...] = reduced
 
     return call(
         kernel,
         (shape_of((count, 128), f32), shape_of((count, parts * rank_part), f32)),
-        (plain, power, gain, slices_own, slices_other, tenants),
+        (plain, power, gain, *slices, tables, *others),
         scalars=(core.reshape(1), chip.reshape(1)),
         in_specs=[
             None,
             None,
             pl.BlockSpec((1, 1, features), lambda step, core, chip: (chip[0], 0, 0)),
-            None,
-            None,
-            None,
-        ],
+        ]
+        + [None] * 3
+        + [pl.BlockSpec(memory_space=pl.ANY)] * len(others),
         flops=2 * features * count * parts * tenant_count * rank_part,
         room=12,
     )
 
 
-def next_gather(left, right, across):
-    half = left.shape[0] // 2
-
-    def kernel(left_ref, right_ref, across_ref, up_ref, down_ref, over_ref):
+def next_gather(own, left, right, across, *others):
+    count, features = left.shape
+    half = count // 2
+
+    def kernel(own_ref, left_ref, right_ref, across_ref, *refs):
+        up_ref, down_ref, over_ref, near_ref = refs[-4:]
         up_ref[:half] = left_ref[:half]
         up_ref[half:] = across_ref[:half]
         down_ref[:half] = right_ref[half:]
         down_ref[half:] = across_ref[half:]
         over_ref[:half] = left_ref[half:]
         over_ref[half:] = right_ref[:half]
+        for index, ref in enumerate((own_ref, left_ref, right_ref, across_ref)):
+            near_ref[:, index * features : (index + 1) * features] = ref[...]
 
     sent = shape_of(left.shape, bf16)
-    return call(kernel, (sent, sent, sent), (left, right, across))
+    return call(
+        kernel,
+        (sent, sent, sent, shape_of((count, 4 * features), bf16)),
+        (own, left, right, across, *others),
+        in_specs=[None] * 4 + [pl.BlockSpec(memory_space=pl.ANY)] * len(others),
+    )
 
 
 def last_gather(up, down, cut):
@@ -364,7 +423,7 @@
     )
 
 
-def project(places, pieces, scale, gain, weights, total=None, finish=None):
+def project(places, pieces, scale, gain, weights, total=None, others=()):
     arrays = []
     layout = []
     for piece in pieces:
@@ -376,7 +435,7 @@
                 known = [len(arrays) - 1]
             entry.append((known[0], start, rows))
         layout.append(entry)
-    count = sum(rows for _, _, rows in pieces[0])
+    count = scale.shape[0]
     query_own, query_other, pairs = weights
     columns = query_own.shape[1]
     chip_width = query_own.shape[0] // 8
@@ -395,12 +454,16 @@
         other_refs = [refs.pop(0) for _ in pieces]
         pair_refs = [refs.pop(0) for _ in pieces]
         total_refs = [refs.pop(0) for _ in range(3)] if has_total else None
-        finish_refs = [refs.pop(0) for _ in range(9)] if finish is not None else None
-        outs, sums = (refs[:-3], refs[-3:]) if finish is not None else ([], refs)
+        sums = refs[-3:]
         step = pl.program_id(0)
         rows = []
         for entry, gain_ref in zip(layout, gain_refs):
-            plain = [taken[at][first : first + size] for at, first, size in entry]
+            plain = [
+                taken[at][:, first : first + chip_width]
+                if size is None
+                else taken[at][first : first + size]
+                for at, first, size in entry
+            ]
             plain = jnp.concatenate(plain, axis=0).astype(f32)
             rows.append((plain * scale_ref[:, :1] * gain_ref[0]).astype(bf16))
         rows = jnp.concatenate(rows, axis=1)
@@ -408,10 +471,7 @@
             result = nn(rows, jnp.concatenate([ref[...] for ref in weight_refs], axis=0))
             if has_total:
                 result += total_refs[side][...]
-            if finish is None:
-                sums[side][...] = result
-            else:
-                sums[side][:, pl.ds(pl.multiple_of(step * part, part), part)] = result
+            sums[side][...] = result
 
         @pl.when(step == 0)
         def _():
@@ -419,12 +479,6 @@
             if has_total:
                 result += total_refs[2][...]
             sums[2][...] = result
-
-        if finish is not None:
-
-            @pl.when(step == steps - 1)
-            def _():
-                finish_kernel(finish_refs, sums, outs)
 
     def weight_spec(index):
         return pl.BlockSpec((chip_width, part), lambda step, places: (places[index], step))
@@ -450,41 +504,60 @@
     if has_total:
         operands += list(total)
         in_specs += list(sum_specs)
-    if finish is None:
-        out_shape, out_specs, scratch = sums, sum_specs, []
-    else:
-        operands += list(finish)
-        in_specs += [None] * 9
-        out_shape = (
-            shape_of((count, 2 * columns), f32),
-            shape_of((count, pairs.shape[0] // 2), bf16),
-            shape_of((count, pairs.shape[0] // 2), bf16),
-        )
-        out_specs = None
-        scratch = [pltpu.VMEM(sum_.shape, f32) for sum_ in sums]
-    return call(
-        kernel,
-        out_shape,
+    operands += list(others)
+    in_specs += [pl.BlockSpec(memory_space=pl.ANY)] * len(others)
+    return call(
+        kernel,
+        sums,
         operands,
         scalars=(places,),
         grid=(steps,),
         in_specs=in_specs,
-        out_specs=out_specs,
-        scratch=scratch,
+        out_specs=sum_specs,
         flops=2 * many * count * chip_width * (2 * columns + pairs.shape[0]),
-        room=28,
-    )
-
-
-def finish_kernel(refs, sums, outs):
-    core_ref, reduced_ref, tenant_ref, own_ref, other_ref, query_gain_ref, key_gain_ref = refs[:7]
-    cosine, sine = refs[7][...], refs[8][...]
+        room=18,
+    )
+
+
+def add(value, piece, *others):
+    def kernel(value_ref, piece_ref, *refs):
+        refs[-1][...] = value_ref[...] + piece_ref[...]
+
+    return call(
+        kernel,
+        shape_of(value.shape, value.dtype),
+        (value, piece, *others),
+        in_specs=[None, None] + [pl.BlockSpec(memory_space=pl.ANY)] * len(others),
+    )
+
+
+def finish(core, query_own, query_other, kv, reduced, got, slices, query_gain, key_gain, tables):
+    count, columns = query_own.shape
+
+    def kernel(core_ref, own_ref, other_ref, kv_ref, *refs):
+        finish_kernel(core_ref, (own_ref, other_ref), kv_ref, refs[:7], refs[7:])
+
+    rows = shape_of((count, kv.shape[1] // 2), bf16)
+    return call(
+        kernel,
+        (shape_of((count, 2 * columns), f32), rows, rows),
+        (query_own, query_other, kv, reduced, got, *slices, query_gain, key_gain, tables),
+        scalars=(core.reshape(1),),
+        flops=2 << 30,
+        room=16,
+    )
+
+
+def finish_kernel(core_ref, query_refs, kv_ref, refs, outs):
+    reduced_ref, got_ref, *slice_refs = refs[:4]
+    query_gain_ref, key_gain_ref, tables_ref = refs[4:]
+    head_size = query_gain_ref.shape[1]
+    cosine, sine = tables_ref[:, :head_size], tables_ref[:, head_size : 2 * head_size]
+    tenant_rows = tables_ref[:, 2 * head_size :]
     out_query_ref, out_key_ref, out_value_ref = outs
-    parts, tenant_count = own_ref.shape[:2]
-    columns = sums[0].shape[1]
-    low_rank = reduced_ref[...].astype(bf16).astype(f32)
-    head_size = cosine.shape[1]
-
+    parts, tenant_count = slice_refs[0].shape[:2]
+    columns = query_refs[0].shape[1]
+    low_rank = (reduced_ref[...] + got_ref[...]).astype(bf16).astype(f32)
     def head_norm(vector, gain):
         power = jnp.mean(vector * vector, axis=-1, keepdims=True)
         vector = vector * lax.rsqrt(power + epsilon) * gain
@@ -492,12 +565,12 @@
 
     spread = jnp.concatenate(
         [
-            jnp.where(tenant_ref[...] == tenant, low_rank, 0.0).astype(bf16)
+            jnp.where(tenant_rows == tenant, low_rank, 0.0).astype(bf16)
             for tenant in range(tenant_count)
         ],
         axis=1,
     )
-    for side, up_ref in enumerate((own_ref, other_ref)):
+    for side, up_ref in enumerate(slice_refs):
         up = jnp.concatenate(
             [
                 up_ref[part, tenant, :, :columns]
@@ -509,12 +582,12 @@
         delta = nn(spread, up)
         for head in range(columns // head_size):
             near = slice(head * head_size, (head + 1) * head_size)
-            query = sums[side][:, near] + adapter_scale * delta[:, near]
+            spot = slice(side * columns + near.start, side * columns + near.stop)
+            query = query_refs[side][:, near] + adapter_scale * delta[:, near]
             query = head_norm(query, query_gain_ref[...])
-            spot = slice(side * columns + near.start, side * columns + near.stop)
             out_query_ref[:, spot] = query.astype(bf16).astype(f32)
-    low = core_ref[0, 0] == 0
-    both = sums[2][...]
+    low = core_ref[0] == 0
+    both = kv_ref[...]
     key = both[:, :head_size].astype(bf16).astype(f32)
     value = both[:, head_size:]
     key = jnp.where(low, key, pltpu.roll(key, head_size // 2, 1))
@@ -612,7 +685,7 @@
         + [cache_spec] * 4
         + [limit_spec],
         out_specs=rows_spec(query_width),
-        room=16,
+        room=10,
         flops=4 * count * query_width * 2 * 2 * block_size,
     )
 
@@ -623,32 +696,42 @@
     depth = own.shape[0]
     chip_width = own.shape[1] // 8
 
-    def kernel(places_ref, attended_ref, own_ref, other_ref, *out_refs):
-        del places_ref
-        weight = jnp.concatenate([own_ref[...], other_ref[...]], axis=0)
-        product = nn(attended_ref[...], weight).astype(bf16)
-        if cut is None:
-            out_refs[0][0] = product
-        else:
-            for ref, start, stop in zip(out_refs, (0, *cut), (*cut, count)):
-                ref[...] = product[start:stop]
-
-    weight_spec = pl.BlockSpec((depth, chip_width), lambda step, places: (0, places[step]))
+    def kernel(places_ref, attended_ref, own_ref, other_ref, *refs):
+        out_refs, (held_ref, arrived) = refs[:-2], refs[-2:]
+        copies = []
+        for step in range(steps):
+            spot = pl.ds(pl.multiple_of(places_ref[step] * chip_width, chip_width), chip_width)
+            for side, weight_ref in enumerate((own_ref, other_ref)):
+                target = held_ref.at[step, side * depth : (side + 1) * depth, :]
+                copy = pltpu.make_async_copy(weight_ref.at[:, spot], target, arrived.at[step, side])
+                copy.start()
+                copies.append(copy)
+        for step in range(steps):
+            copies[2 * step].wait()
+            copies[2 * step + 1].wait()
+            product = nn(attended_ref[...], held_ref[step]).astype(bf16)
+            if cut is None:
+                out_refs[0][step] = product
+            else:
+                for ref, start, stop in zip(out_refs, (0, *cut), (*cut, count)):
+                    ref[...] = product[start:stop]
+
     if cut is None:
         out_shape = shape_of((steps, count, chip_width), bf16)
-        out_specs = pl.BlockSpec((1, count, chip_width), lambda step, places: (step, 0, 0))
     else:
         sizes = (cut[0], cut[1] - cut[0], count - cut[1])
         out_shape = tuple(shape_of((size, chip_width), bf16) for size in sizes)
-        out_specs = None
+    in_hbm = pl.BlockSpec(memory_space=pltpu.HBM)
     return call(
         kernel,
         out_shape,
         (attended, own, other),
         scalars=(places,),
-        grid=(steps,),
-        in_specs=[None, weight_spec, weight_spec],
-        out_specs=out_specs,
+        in_specs=[None, in_hbm, in_hbm],
+        scratch=[
+            pltpu.VMEM((steps, 2 * depth, chip_width), bf16),
+            pltpu.SemaphoreType.DMA((steps, 2)),
+        ],
         flops=2 * steps * count * width * chip_width,
         room=16,
     )
@@ -771,51 +854,31 @@
     own_width = embedding.shape[1]
     chip_width = 2 * own_width
     head_size = query_norm_gain.shape[0]
-    half_dim = head_size // 2
-    tenant_count, _, rank_part = adapter_down_weight.shape
     me = lax.axis_index("rep")
     tp = lax.axis_index("tp")
     core = tp % 2
     chip = tp // 2
 
     packed = jnp.concatenate([adapter_up_weight, adapter_down_weight.transpose(0, 2, 1)], axis=2)
+    slices_own = over_replicas(packed)
     key_own, value_own = key_weight.T, value_weight.T
-    before = (
-        over_replicas(packed),
-        to_partner(query_weight),
-        to_partner(key_own),
-        to_partner(value_own),
-    )
-
-    def beside(before):
-        slices, query_other, key_other, value_other = before
-        mine = core * half_rows
-        lengths = lax.dynamic_slice_in_dim(stored_lengths, mine, half_rows, 0)
-        tenants = lax.dynamic_slice_in_dim(row_tenant_index, mine, half_rows, 0)
-        tenants = jnp.repeat(tenants, step_count)[:, None]
-        positions = (lengths[:, None] + jnp.arange(step_count)).reshape(count)
-        cosine, sine = rope_tables(positions, half_dim)
-        return (
-            slices,
-            to_partner(slices),
-            query_other,
-            jnp.concatenate([key_own, key_other, value_own, value_other]),
-            to_partner(stored_keys),
-            to_partner(stored_values),
-            to_partner(output_weight),
-            tenants,
-            jnp.concatenate([cosine, cosine], axis=1),
-            jnp.concatenate([-sine, sine], axis=1),
-            input_norm_gain.reshape(8, 1, chip_width),
-        )
+    query_other = to_partner(query_weight)
+    output_other = to_partner(output_weight)
+    pair_other = to_partner(jnp.concatenate([key_own, value_own]))
+    keys_other, values_other = to_partner(stored_keys), to_partner(stored_values)
+    gain = input_norm_gain.reshape(8, 1, chip_width)
+
+    def beside(sent):
+        tables = row_tables(core, stored_lengths, row_tenant_index, step_count, head_size, sent)
+        pairs = stack_pairs(key_own, value_own, pair_other, sent)
+        slices = after(slices_own, sent)
+        slices_other = to_partner(slices)
+        return tables, slices, slices_other, pairs, query_other, keys_other, values_other, output_other
 
     tokens = step_token_index.reshape(step_count, replica_count, 2, half_rows)
     tokens = tokens.transpose(1, 2, 3, 0).reshape(replica_count, 2 * count)
-    held, beside = embed(tokens, embedding.T, me, before, beside)
-    slices, slices_other, query_other, pairs, keys_other, values_other, output_other = beside[:7]
-    tenants, cosine, sine, gain = beside[7:]
-    kept = lax.dynamic_index_in_dim(held, core, 0, keepdims=False)
-    passed = lax.dynamic_index_in_dim(held, 1 - core, 0, keepdims=False)
+    kept, passed, beside = embed(tokens, embedding.T, me, core, slices_own, beside)
+    tables, *slices, pairs = beside[:4]
     own, power = to_rows(core, kept, to_partner(passed))
 
     z, y = chip // 4, chip % 4
@@ -827,52 +890,53 @@
     third = count // 3 // 16 * 16
     cut = (third, 2 * third)
     left, right, across = to_tp(own, 0, 1), to_tp(own, 0, -1), to_tp(own, 1, 0)
-    power = across_chips(power)
-    scale, reduced = reduce_own(core, chip, own, power, gain, slices, slices_other, tenants)
-    reduced = across_chips(reduced)
-    up, down, over = next_gather(left, right, across)
+    power = power + to_tp(power, 1, 0)
+    up, down, over, near = next_gather(own, left, right, across, power)
+    power = after(power, over)
     up, down, over = to_tp(up, 0, 1), to_tp(down, 0, -1), to_tp(over, 1, 0)
+    for mask in (1, 3):
+        power = power + to_other_side(power, mask)
+    last_up, last_down, last_over = last_gather(up, down, cut)
+    scale, reduced = reduce_own(core, chip, own, power, gain, slices, tables, last_over)
+    last_up, last_down = to_tp(last_up, 0, 1), to_tp(last_down, 0, -1)
+    last_over = to_tp(last_over, 1, 0)
+    reduced = reduced + to_tp(reduced, 1, 0)
+    got = to_other_side(reduced, 1)
     weights = (query_weight, query_other, pairs)
     total = project(
         places((0, 0), (0, -1), (0, 1), (1, 0)),
-        [[(own, 0, count)], [(left, 0, count)], [(right, 0, count)], [(across, 0, count)]],
+        [[(near, index * chip_width, None)] for index in range(4)],
         scale,
         gain,
         weights,
     )
-    last_up, last_down, last_over = last_gather(up, down, cut)
-    last_up, last_down = to_tp(last_up, 0, 1), to_tp(last_down, 0, -1)
-    last_over = to_tp(last_over, 1, 0)
-    total = project(
-        places((0, 2), (1, -1), (1, 1)),
+    reduced = add(reduced, got, total[2])
+    got = to_other_side(reduced, 3)
+    query_a, query_b, kv = project(
+        places((0, 2), (1, -1), (1, 1), (1, 2)),
         [
             [(up, 0, half), (down, 0, half)],
             [(up, half, half), (over, 0, half)],
             [(over, half, half), (down, half, half)],
+            [(last_up, 0, third), (last_over, 0, third), (last_down, 0, count - 2 * third)],
         ],
         scale,
         gain,
         weights,
         total,
-    )
-    query, new_keys, new_values = project(
-        places((1, 2)),
-        [[(last_up, 0, third), (last_over, 0, third), (last_down, 0, count - 2 * third)]],
-        scale,
-        gain,
-        weights,
-        total,
-        (
-            core.reshape(1, 1),
-            reduced,
-            tenants,
-            slices,
-            slices_other,
-            query_norm_gain[None],
-            key_norm_gain[None],
-            cosine,
-            sine,
-        ),
+        (reduced,),
+    )
+    query, new_keys, new_values = finish(
+        core,
+        query_a,
+        query_b,
+        kv,
+        reduced,
+        got,
+        slices,
+        query_norm_gain[None],
+        key_norm_gain[None],
+        tables,
     )
 
     attended = attend(

time: 169 us -> 162 us (0.959)
  starting transfers between devices: 60.5 us -> 56.9 us
  other arithmetic: 7.14 us -> 4.39 us
  local copies, waits for them, and re-layouts: 17 us -> 18.9 us
    unnamed x70 -> x80, local copies, waits for them, and re-layouts: 12.2 us -> 17.5 us
    all_to_all x1, waiting for transfers between devices: 9.81 us -> 5.12 us  [embed(): got = lax.all_to_all(sent, 'rep', 0, 0, tiled=True)]
    ppermute x20, waiting for transfers between devices: 11.1 us -> 15.2 us  [to_tp(): return lax.ppermute(block, 'tp', tp_route(dz, dy, 0))]
    ppermute x4, starting transfers between devices: 5.33 us -> 2.86 us  [to_other_side(): return lax.ppermute(value, 'tp', route)]
    ppermute x4, waiting for transfers between devices: 6.73 us -> 4.92 us  [to_other_side(): return lax.ppermute(value, 'tp', route)]
    ppermute x9 -> x8, starting transfers between devices: 14.8 us -> 13.5 us  [to_partner(): return lax.ppermute(block, 'tp', tp_route(0, 0, 1))]
    pallas_call x18 -> x21, Pallas kernels: 51 us -> 50.3 us  [call(): pl.pallas_call(kernel, out_shape=out_shape, grid_spec=pltpu.PrefetchScala...]
  transfers between devices with their start and end apart: 35 -> 34, of which waited for: 11 -> 10; matrix products, arithmetic and copies ran while one was open for 7% -> 4% of each run, Pallas kernels for 19% -> 20%
where the time goes in v2:
time: 162 us; the launch traced here: 161 us
  starting transfers between devices  56.9 us (35%)
  Pallas kernels  50.3 us (31%)
  waiting for transfers between devices  29.3 us (18%)
  local copies, waits for them, and re-layouts  18.9 us (12%)
  other arithmetic  4.39 us (3%)
    pallas_call x21, Pallas kernels, call(): pl.pallas_call(kernel, out_shape=out_shape, grid_spec=pltpu.PrefetchScala...  50.3 us
    ppermute x20, starting transfers between devices, to_tp(): return lax.ppermute(block, 'tp', tp_route(dz, dy, 0))  30.8 us
    unnamed x80, local copies, waits for them, and re-layouts  17.5 us
    ppermute x20, waiting for transfers between devices, to_tp(): return lax.ppermute(block, 'tp', tp_route(dz, dy, 0))  15.2 us
    ppermute x8, starting transfers between devices, to_partner(): return lax.ppermute(block, 'tp', tp_route(0, 0, 1))  13.5 us
    all_to_all x1, starting transfers between devices, over_replicas(): return lax.all_to_all(copies, 'rep', 0, 0, tiled=True)  5.47 us
    all_to_all x1, waiting for transfers between devices, embed(): got = lax.all_to_all(sent, 'rep', 0, 0, tiled=True)  5.12 us
    ppermute x4, waiting for transfers between devices, to_other_side(): return lax.ppermute(value, 'tp', route)  4.92 us
  transfers between devices with their start and end apart: 34, of which 10 were waited for; matrix products, arithmetic and copies ran while one was open for 4% of the time, Pallas kernels for 20%

profile of v2, /device:TPU:1, one launch (start us, length us, event | category | flops | bytes accessed | tf_op | source)
XLA Modules:
  0.0 161.1 jit_solution(1529404553547282079)
XLA Ops:
  1.9 2.4 %pad_maximum_fusion = bf16[128,5120]{1,0:T(8,128)(2,1)} fusion(bf16[64,5120]{1,0:T(8,128)(2,1)} %bitcast.41, bf16[64,5120]{1,0:T(8,128)(2,1)} %bitcast.39), kind=kLoop, calls=%fused_computation | loop fusion | flops 2621440 | bytes 2621440 | tf_op jit(solution)/shard_map/concatenate | solution.py:867
  5.9 5.5 %all-to-all-start.1 = ((bf16[8,4,16,832]{3,2,1,0:T(8,128)(2,1)}), bf16[8,4,16,832]{3,2,1,0:T(8,128)(2,1)S(1)}, u32[]{:S(2)}, u32[]{:S(2)}) async-start(bf16[8,4,16,832]{3,2,1,0:T(8,128)(2,1)} %broadcast_in_dim.18), calls=%async_computation.1 | async-start | bytes 1835008 | tf_op jit(solution)/shard_map/all_to_all | solution.py:39
  13.1 10.2 %shard_map.164.refs_0_ = bf16[8,320,128]{2,1,0:T(8,128)(2,1)S(1)} custom-call(s32[1]{0:T(128)} %bitcast.13.me_ref, s32[1]{0:T(128)} %constant.136.clone.1.base_ref, s32[8,512]{1,0:T(8,128)S(1)} %copy.23.tokens_ref, s32[16,512]{1,0:T(8,128)S(1)} %get-tuple-element.222.rank_ref, bf16[320,9496]{1,0:T(8,128)(2,1)} %bitcast.58), custom_call_target="tpu_custom_call" | custom-call | flops 6223298560 | bytes 6126592 | tf_op jit(solution)/shard_map/pallas_call | solution.py:74
  27.7 4.2 %all-to-all-start.2 = ((bf16[8,320,128]{2,1,0:T(8,128)(2,1)}), bf16[8,320,128]{2,1,0:T(8,128)(2,1)}, u32[]{:S(2)}, u32[]{:S(2)}) async-start(bf16[8,320,128]{2,1,0:T(8,128)(2,1)} %shard_map.165.refs_0_.refs_1_.ready_ref), calls=%async_computation.2 | async-start | bytes 1310720 | tf_op jit(solution)/shard_map/all_to_all | solution.py:274
  38.5 5.1 %all-to-all-done.2.got_ref = bf16[8,320,128]{2,1,0:T(8,128)(2,1)} async-done(((bf16[8,320,128]{2,1,0:T(8,128)(2,1)}), bf16[8,320,128]{2,1,0:T(8,128)(2,1)}, u32[]{:S(2)}, u32[]{:S(2)}) %all-to-all-start.2) | async-done | bytes 655392 | tf_op jit(solution)/shard_map/all_to_all | solution.py:274
  44.7 2.7 %shard_map.169 = (bf16[320,256]{1,0:T(8,128)(2,1)}, bf16[320,256]{1,0:T(8,128)(2,1)}) custom-call(s32[1]{0:T(128)} %bitcast.4.core_ref, s32[1]{0:T(128)} %constant.136.clone.1.base_ref, s32[16,512]{1,0:T(8,128)} %copy-done.35, bf16[8,320,128]{2,1,0:T(8,128)(2,1)} %all-to-all-done.2.got_ref, f32[256,384]{1,0:T(8,128)S(1)} %copy-done.9, ...), custom_call_target="tpu_custom_call" | custom-call | flops 1048576 | bytes 22183936 | tf_op jit(solution)/shard_map/pallas_call | solution.py:74
  54.1 3.3 %collective-permute-start.9 = (bf16[256,640]{1,0:T(8,128)(2,1)S(1)}, bf16[256,640]{1,0:T(8,128)(2,1)S(1)}, u32[]{:S(2)}, u32[]{:S(2)}) collective-permute-start(bf16[256,640]{1,0:T(8,128)(2,1)S(1)} %get-tuple-element.97.own_ref.plain_ref), channel_id=1, source_target_pairs={{0,8},{1,9},{2,10},{3,11},{4,12},{5,13},{6,14},{7,15},{8,0},{9,1},... | collective-permute-start | bytes 983048 | tf_op jit(solution)/shard_map/ppermute | solution.py:29
  57.5 7.3 %collective-permute-done.10 = f32[2,128]{1,0:T(2,128)S(1)} collective-permute-done((f32[2,128]{1,0:T(2,128)S(1)}, f32[2,128]{1,0:T(2,128)S(1)}, u32[]{:S(2)}, u32[]{:S(2)}) %collective-permute-start.10) | collective-permute-done | bytes 1056 | tf_op jit(solution)/shard_map/ppermute | solution.py:29
  66.8 2.7 %collective-permute-start.12 = (bf16[256,640]{1,0:T(8,128)(2,1)S(1)}, bf16[256,640]{1,0:T(8,128)(2,1)S(1)}, u32[]{:S(2)}, u32[]{:S(2)}) collective-permute-start(bf16[256,640]{1,0:T(8,128)(2,1)S(1)} %get-tuple-element.100), channel_id=1, source_target_pairs={{0,6},{1,7},{2,0},{3,1},{4,2},{5,3},{6,4},{7,5},{8,14},{9,15},{10,... | collective-permute-start | bytes 983048 | tf_op jit(solution)/shard_map/ppermute | solution.py:29
  69.5 4.9 %collective-permute-done.17 = f32[2,128]{1,0:T(2,128)S(1)} collective-permute-done((f32[2,128]{1,0:T(2,128)}, f32[2,128]{1,0:T(2,128)S(1)}, u32[]{:S(2)}, u32[]{:S(2)}) %collective-permute-start.17) | collective-permute-done | bytes 1056 | tf_op jit(solution)/shard_map/ppermute | solution.py:327
  80.0 2.6 %shard_map.174 = (f32[256,128]{1,0:T(8,128)S(1)}, f32[256,128]{1,0:T(8,128)}) custom-call(s32[1]{0:T(128)} %bitcast.4.core_ref, s32[1]{0:T(128)} %bitcast.22.chip_ref, bf16[256,640]{1,0:T(8,128)(2,1)S(1)} %get-tuple-element.97.own_ref.plain_ref, f32[2,128]{1,0:T(2,128)S(1)} %add.156.power_ref, f32[8,1,640]{2,1,0:T(1,128)S(1)} %bitcast.43, ...), custom_call_target="tpu_custom_call" | custom-call | flops 167772160 | bytes 2548736 | tf_op jit(solution)/shard_map/pallas_call | solution.py:74
  90.6 2.5 %copy-done = bf16[5120,512]{1,0:T(8,128)(2,1)S(1)} copy-done((bf16[5120,512]{1,0:T(8,128)(2,1)S(1)}, bf16[5120,512]{1,0:T(8,128)(2,1)}, u32[]{:S(2)}) %copy-start) | copy-done | bytes 5242904
  96.2 4.9 %shard_map.175 = (f32[256,512]{1,0:T(8,128)S(1)}, f32[256,512]{1,0:T(8,128)S(1)}, f32[256,256]{1,0:T(8,128)S(1)}) custom-call(s32[4]{0:T(128)S(1)} %pad_add_fusion.2.places_ref, bf16[256,2560]{1,0:T(8,128)(2,1)S(1)} %copy-done.17, f32[256,128]{1,0:T(8,128)S(1)} %get-tuple-element.105.refs_1_.refs_6_, f32[8,1,640]{2,1,0:T(1,128)S(1)} %bitcast.44, ...), custom_call_target="tpu_custom_call" | custom-call | flops 1677721600 | bytes 53952512 | tf_op jit(solution)/shard_map/pallas_call | solution.py:74
  102.1 4.9 %shard_map.177 = (f32[256,512]{1,0:T(8,128)S(1)}, f32[256,512]{1,0:T(8,128)S(1)}, f32[256,256]{1,0:T(8,128)S(1)}) custom-call(s32[4]{0:T(128)S(1)} %pad_add_fusion.1.places_ref, bf16[256,640]{1,0:T(8,128)(2,1)S(1)} %collective-permute-done.11.up_ref.refs_0_, bf16[256,640]{1,0:T(8,128)(2,1)S(1)} %collective-permute-done.12.down_ref.refs_1_, ...), custom_call_target="tpu_custom_call" | custom-call | flops 1677721600 | bytes 55394304 | tf_op jit(solution)/shard_map/pallas_call | solution.py:74
  107.1 2.8 %shard_map.178 = (f32[256,1024]{1,0:T(8,128)S(1)}, bf16[256,128]{1,0:T(8,128)(2,1)S(1)}, bf16[256,128]{1,0:T(8,128)(2,1)S(1)}) custom-call(s32[1]{0:T(128)} %bitcast.4.core_ref, f32[256,512]{1,0:T(8,128)S(1)} %get-tuple-element.111.own_ref, f32[256,512]{1,0:T(8,128)S(1)} %get-tuple-element.112.other_ref, f32[256,256]{1,0:T(8,128)S(1)} %get-tuple-element.113.kv_ref, ...), custom_call_target="tpu_custom_call" | custom-call | flops 2147483648 | bytes 3671040 | tf_op jit(solution)/shard_map/pallas_call | solution.py:74
  109.9 7.7 %shard_map.179.attended_ref = bf16[256,1024]{1,0:T(8,128)(2,1)S(1)} custom-call(s32[1]{0:T(128)} %bitcast.4.core_ref, s32[128]{0:T(128)S(1)} %copy-done.24, f32[256,1024]{1,0:T(8,128)S(1)} %get-tuple-element.114.query_ref, bf16[256,128]{1,0:T(8,128)(2,1)S(1)} %get-tuple-element.115.new_key_ref, bf16[256,128]{1,0:T(8,128)(2,1)S(1)} %get-tuple-element.116.new_value_ref, ...), custom_call_target="tpu_custom_call" | custom-call | flops 402653184 | bytes 14172160 | tf_op jit(solution)/shard_map/pallas_call | solution.py:74
  122.2 2.5 %collective-permute-start.24 = (bf16[96,640]{1,0:T(8,128)(2,1)S(1)}, bf16[96,640]{1,0:T(8,128)(2,1)S(1)}, u32[]{:S(2)}, u32[]{:S(2)}) collective-permute-start(bf16[96,640]{1,0:T(8,128)(2,1)S(1)} %get-tuple-element.119), channel_id=1, source_target_pairs={{0,8},{1,9},{2,10},{3,11},{4,12},{5,13},{6,14},{7,15},{8,0},{9,1},... | collective-permute-start | bytes 368648 | tf_op jit(solution)/shard_map/ppermute | solution.py:29
  124.7 3.5 %shard_map.181.blocks_ref = bf16[3,256,640]{2,1,0:T(8,128)(2,1)S(1)} custom-call(s32[3]{0:T(128)S(1)} %pad_add_fusion.3.places_ref, bf16[256,1024]{1,0:T(8,128)(2,1)S(1)} %shard_map.179.attended_ref, bf16[512,5120]{1,0:T(8,128)(2,1)S(1)} %bitcast.38, bf16[512,5120]{1,0:T(8,128)(2,1)} %collective-permute-done.5.refs_7_.other_ref), custom_call_target="tpu_custom_call" | custom-call | flops 1006632960 | bytes 11010048 | tf_op jit(solution)/shard_map/pallas_call | solution.py:74
  128.5 2.7 %collective-permute-start.26 = (bf16[256,640]{1,0:T(8,128)(2,1)S(1)}, bf16[256,640]{1,0:T(8,128)(2,1)S(1)}, u32[]{:S(2)}, u32[]{:S(2)}) collective-permute-start(bf16[256,640]{1,0:T(8,128)(2,1)S(1)} %get-tuple-element.121), channel_id=1, source_target_pairs={{0,6},{1,7},{2,0},{3,1},{4,2},{5,3},{6,4},{7,5},{8,14},{9,15},{10,... | collective-permute-start | bytes 983048 | tf_op jit(solution)/shard_map/ppermute | solution.py:29
  132.8 4.1 %shard_map.180.blocks_ref = bf16[4,256,640]{2,1,0:T(8,128)(2,1)S(1)} custom-call(s32[4]{0:T(128)S(1)} %pad_add_fusion.places_ref, bf16[256,1024]{1,0:T(8,128)(2,1)S(1)} %shard_map.179.attended_ref, bf16[512,5120]{1,0:T(8,128)(2,1)S(1)} %bitcast.38, bf16[512,5120]{1,0:T(8,128)(2,1)} %collective-permute-done.5.refs_7_.other_ref), custom_call_target="tpu_custom_call" | custom-call | flops 1342177280 | bytes 11010048 | tf_op jit(solution)/shard_map/pallas_call | solution.py:74
  138.9 2.7 %collective-permute-start.29 = (bf16[256,640]{1,0:T(8,128)(2,1)S(1)}, bf16[256,640]{1,0:T(8,128)(2,1)S(1)}, u32[]{:S(2)}, u32[]{:S(2)}) collective-permute-start(bf16[256,640]{1,0:T(8,128)(2,1)S(1)} %get-tuple-element.124), channel_id=1, source_target_pairs={{0,6},{1,7},{2,0},{3,1},{4,2},{5,3},{6,4},{7,5},{8,14},{9,15},{10,... | collective-permute-start | bytes 983048 | tf_op jit(solution)/shard_map/ppermute | solution.py:29
  143.2 2.8 %collective-permute-done.28.up_ref = bf16[256,640]{1,0:T(8,128)(2,1)S(1)} collective-permute-done((bf16[256,640]{1,0:T(8,128)(2,1)S(1)}, bf16[256,640]{1,0:T(8,128)(2,1)S(1)}, u32[]{:S(2)}, u32[]{:S(2)}) %collective-permute-start.28) | collective-permute-done | bytes 327712 | tf_op jit(solution)/shard_map/ppermute | solution.py:29
  146.0 3.0 %collective-permute-done.30.over_ref = bf16[256,640]{1,0:T(8,128)(2,1)S(1)} collective-permute-done((bf16[256,640]{1,0:T(8,128)(2,1)S(1)}, bf16[256,640]{1,0:T(8,128)(2,1)S(1)}, u32[]{:S(2)}, u32[]{:S(2)}) %collective-permute-start.30) | collective-permute-done | bytes 327712 | tf_op jit(solution)/shard_map/ppermute | solution.py:29
  149.4 9.4 %collective-permute-start.31 = (bf16[256,320]{1,0:T(8,128)(2,1)S(1)}, bf16[256,320]{1,0:T(8,128)(2,1)S(1)}, u32[]{:S(2)}, u32[]{:S(2)}) collective-permute-start(bf16[256,320]{1,0:T(8,128)(2,1)S(1)} %get-tuple-element.127), channel_id=1, source_target_pairs={{0,1},{1,0},{2,3},{3,2},{4,5},{5,4},{6,7},{7,6},{8,9},{9,8},{10,11... | collective-permute-start | bytes 491528 | tf_op jit(solution)/shard_map/ppermute | solution.py:33
  (165 shorter events, 56.0 us)
Async XLA Ops:
  0.0 43.6 %collective-permute-start.2 = (bf16[5120,512]{1,0:T(8,128)(2,1)}, bf16[5120,512]{1,0:T(8,128)(2,1)}, u32[]{:S(2)}, u32[]{:S(2)}) collective-permute-start(bf16[5120,512]{1,0:T(8,128)(2,1)} %refs_14_.1), channel_id=1, source_target_pairs={{0,1},{1,0},{2,3},{3,2},{4,5},{5,4},{6,7},{7,6},{8,9},{9,8},{10,11... | collective-permute-start | bytes 15728648 | tf_op jit(solution)/shard_map/ppermute | solution.py:33
  1.4 42.2 %collective-permute-start.5 = (bf16[512,5120]{1,0:T(8,128)(2,1)}, bf16[512,5120]{1,0:T(8,128)(2,1)}, u32[]{:S(2)}, u32[]{:S(2)}) collective-permute-start(bf16[512,5120]{1,0:T(8,128)(2,1)} %own_ref.5), channel_id=1, source_target_pairs={{0,1},{1,0},{2,3},{3,2},{4,5},{5,4},{6,7},{7,6},{8,9},{9,8},{10,11... | collective-permute-start | bytes 15728648 | tf_op jit(solution)/shard_map/ppermute | solution.py:33
  1.4 42.2 %collective-permute-start.3 = (bf16[128,96,128]{2,1,0:T(8,128)(2,1)}, bf16[128,96,128]{2,1,0:T(8,128)(2,1)}, u32[]{:S(2)}, u32[]{:S(2)}) collective-permute-start(bf16[128,96,128]{2,1,0:T(8,128)(2,1)} %own_key_ref.1), channel_id=1, source_target_pairs={{0,1},{1,0},{2,3},{3,2},{4,5},{5,4},{6,7},{7,6},{8,9},{9,8},{10,11... | collective-permute-start | bytes 9437192 | tf_op jit(solution)/shard_map/ppermute | solution.py:33
  1.9 41.7 %collective-permute-start.4 = (bf16[128,96,128]{2,1,0:T(8,128)(2,1)}, bf16[128,96,128]{2,1,0:T(8,128)(2,1)}, u32[]{:S(2)}, u32[]{:S(2)}) collective-permute-start(bf16[128,96,128]{2,1,0:T(8,128)(2,1)} %own_value_ref.1), channel_id=1, source_target_pairs={{0,1},{1,0},{2,3},{3,2},{4,5},{5,4},{6,7},{7,6},{8,9},{9,8},{10,11... | collective-permute-start | bytes 9437192 | tf_op jit(solution)/shard_map/ppermute | solution.py:33
  4.4 22.5 %collective-permute-start.1 = (bf16[128,5120]{1,0:T(8,128)(2,1)}, bf16[128,5120]{1,0:T(8,128)(2,1)S(1)}, u32[]{:S(2)}, u32[]{:S(2)}) collective-permute-start(bf16[128,5120]{1,0:T(8,128)(2,1)} %pad_maximum_fusion), channel_id=1, source_target_pairs={{0,1},{1,0},{2,3},{3,2},{4,5},{5,4},{6,7},{7,6},{8,9},{9,8},{10,11... | collective-permute-start | bytes 3932168 | tf_op jit(solution)/shard_map/ppermute | solution.py:33
  5.9 20.0 %all-to-all-start.1 = ((bf16[8,4,16,832]{3,2,1,0:T(8,128)(2,1)}), bf16[8,4,16,832]{3,2,1,0:T(8,128)(2,1)S(1)}, u32[]{:S(2)}, u32[]{:S(2)}) async-start(bf16[8,4,16,832]{3,2,1,0:T(8,128)(2,1)} %broadcast_in_dim.18), calls=%async_computation.1 | async-start | bytes 1835008 | tf_op jit(solution)/shard_map/all_to_all | solution.py:39
  26.9 16.8 %collective-permute-start = (bf16[8,4,16,832]{3,2,1,0:T(8,128)(2,1)}, bf16[8,4,16,832]{3,2,1,0:T(8,128)(2,1)}, u32[]{:S(2)}, u32[]{:S(2)}) collective-permute-start(bf16[8,4,16,832]{3,2,1,0:T(8,128)(2,1)} %shard_map.167.refs_1_.own_ref.refs_2_), channel_id=1, source_target_pairs={{0,1},{1,0},{2,3},{3,2},{4,5},{5,4},{6,7},{7,6},{8,9},{9,8},{10,11... | collective-permute-start | bytes 2555912 | tf_op jit(solution)/shard_map/ppermute | solution.py:33
  27.7 15.9 %all-to-all-start.2 = ((bf16[8,320,128]{2,1,0:T(8,128)(2,1)}), bf16[8,320,128]{2,1,0:T(8,128)(2,1)}, u32[]{:S(2)}, u32[]{:S(2)}) async-start(bf16[8,320,128]{2,1,0:T(8,128)(2,1)} %shard_map.165.refs_0_.refs_1_.ready_ref), calls=%async_computation.2 | async-start | bytes 1310720 | tf_op jit(solution)/shard_map/all_to_all | solution.py:274
  51.2 13.5 %collective-permute-start.7 = (bf16[256,640]{1,0:T(8,128)(2,1)S(1)}, bf16[256,640]{1,0:T(8,128)(2,1)S(1)}, u32[]{:S(2)}, u32[]{:S(2)}) collective-permute-start(bf16[256,640]{1,0:T(8,128)(2,1)S(1)} %get-tuple-element.97.own_ref.plain_ref), channel_id=1, source_target_pairs={{0,2},{1,3},{2,4},{3,5},{4,6},{5,7},{6,0},{7,1},{8,10},{9,11},{10,... | collective-permute-start | bytes 983048 | tf_op jit(solution)/shard_map/ppermute | solution.py:29
  52.6 12.2 %collective-permute-start.8 = (bf16[256,640]{1,0:T(8,128)(2,1)S(1)}, bf16[256,640]{1,0:T(8,128)(2,1)S(1)}, u32[]{:S(2)}, u32[]{:S(2)}) collective-permute-start(bf16[256,640]{1,0:T(8,128)(2,1)S(1)} %get-tuple-element.97.own_ref.plain_ref), channel_id=1, source_target_pairs={{0,6},{1,7},{2,0},{3,1},{4,2},{5,3},{6,4},{7,5},{8,14},{9,15},{10,... | collective-permute-start | bytes 983048 | tf_op jit(solution)/shard_map/ppermute | solution.py:29
  54.1 10.6 %collective-permute-start.9 = (bf16[256,640]{1,0:T(8,128)(2,1)S(1)}, bf16[256,640]{1,0:T(8,128)(2,1)S(1)}, u32[]{:S(2)}, u32[]{:S(2)}) collective-permute-start(bf16[256,640]{1,0:T(8,128)(2,1)S(1)} %get-tuple-element.97.own_ref.plain_ref), channel_id=1, source_target_pairs={{0,8},{1,9},{2,10},{3,11},{4,12},{5,13},{6,14},{7,15},{8,0},{9,1},... | collective-permute-start | bytes 983048 | tf_op jit(solution)/shard_map/ppermute | solution.py:29
  66.8 11.9 %collective-permute-start.11 = (bf16[256,640]{1,0:T(8,128)(2,1)S(1)}, bf16[256,640]{1,0:T(8,128)(2,1)S(1)}, u32[]{:S(2)}, u32[]{:S(2)}) collective-permute-start(bf16[256,640]{1,0:T(8,128)(2,1)S(1)} %get-tuple-element.99), channel_id=1, source_target_pairs={{0,2},{1,3},{2,4},{3,5},{4,6},{5,7},{6,0},{7,1},{8,10},{9,11},{10,... | collective-permute-start | bytes 983048 | tf_op jit(solution)/shard_map/ppermute | solution.py:29
  66.8 11.9 %collective-permute-start.12 = (bf16[256,640]{1,0:T(8,128)(2,1)S(1)}, bf16[256,640]{1,0:T(8,128)(2,1)S(1)}, u32[]{:S(2)}, u32[]{:S(2)}) collective-permute-start(bf16[256,640]{1,0:T(8,128)(2,1)S(1)} %get-tuple-element.100), channel_id=1, source_target_pairs={{0,6},{1,7},{2,0},{3,1},{4,2},{5,3},{6,4},{7,5},{8,14},{9,15},{10,... | collective-permute-start | bytes 983048 | tf_op jit(solution)/shard_map/ppermute | solution.py:29
  76.3 25.7 %collective-permute-start.13 = (bf16[256,640]{1,0:T(8,128)(2,1)}, bf16[256,640]{1,0:T(8,128)(2,1)}, u32[]{:S(2)}, u32[]{:S(2)}) collective-permute-start(bf16[256,640]{1,0:T(8,128)(2,1)} %copy-done.21), channel_id=1, source_target_pairs={{0,8},{1,9},{2,10},{3,11},{4,12},{5,13},{6,14},{7,15},{8,0},{9,1},... | collective-permute-start | bytes 983048 | tf_op jit(solution)/shard_map/ppermute | solution.py:29
  85.2 16.9 %collective-permute-start.15 = (bf16[80,640]{1,0:T(8,128)(2,1)}, bf16[80,640]{1,0:T(8,128)(2,1)S(1)}, u32[]{:S(2)}, u32[]{:S(2)}) collective-permute-start(bf16[80,640]{1,0:T(8,128)(2,1)} %copy-done.22), channel_id=1, source_target_pairs={{0,8},{1,9},{2,10},{3,11},{4,12},{5,13},{6,14},{7,15},{8,0},{9,1},... | collective-permute-start | bytes 307208 | tf_op jit(solution)/shard_map/ppermute | solution.py:29
  85.8 16.2 %collective-permute-start.14 = (bf16[80,640]{1,0:T(8,128)(2,1)}, bf16[80,640]{1,0:T(8,128)(2,1)S(1)}, u32[]{:S(2)}, u32[]{:S(2)}) collective-permute-start(bf16[80,640]{1,0:T(8,128)(2,1)} %copy-done.28), channel_id=1, source_target_pairs={{0,2},{1,3},{2,4},{3,5},{4,6},{5,7},{6,0},{7,1},{8,10},{9,11},{10,... | collective-permute-start | bytes 307208 | tf_op jit(solution)/shard_map/ppermute | solution.py:29
  86.4 15.6 %collective-permute-start.16 = (bf16[96,640]{1,0:T(8,128)(2,1)}, bf16[96,640]{1,0:T(8,128)(2,1)S(1)}, u32[]{:S(2)}, u32[]{:S(2)}) collective-permute-start(bf16[96,640]{1,0:T(8,128)(2,1)} %copy-done.27), channel_id=1, source_target_pairs={{0,6},{1,7},{2,0},{3,1},{4,2},{5,3},{6,4},{7,5},{8,14},{9,15},{10,... | collective-permute-start | bytes 368648 | tf_op jit(solution)/shard_map/ppermute | solution.py:29
  89.9 11.2 %collective-permute-start.20 = (f32[256,128]{1,0:T(8,128)S(1)}, f32[256,128]{1,0:T(8,128)S(1)}, u32[]{:S(2)}, u32[]{:S(2)}) collective-permute-start(f32[256,128]{1,0:T(8,128)S(1)} %add.157.value_ref), channel_id=1, source_target_pairs={{0,2},{1,3},{2,0},{3,1},{4,6},{5,7},{6,4},{7,5},{8,10},{9,11},{10,... | collective-permute-start | bytes 393224 | tf_op jit(solution)/shard_map/ppermute | solution.py:327
  119.4 8.8 %collective-permute-start.22 = (bf16[80,640]{1,0:T(8,128)(2,1)S(1)}, bf16[80,640]{1,0:T(8,128)(2,1)S(1)}, u32[]{:S(2)}, u32[]{:S(2)}) collective-permute-start(bf16[80,640]{1,0:T(8,128)(2,1)S(1)} %get-tuple-element.117), channel_id=1, source_target_pairs={{0,2},{1,3},{2,4},{3,5},{4,6},{5,7},{6,0},{7,1},{8,10},{9,11},{10,... | collective-permute-start | bytes 307208 | tf_op jit(solution)/shard_map/ppermute | solution.py:29
  120.4 7.9 %collective-permute-start.23 = (bf16[80,640]{1,0:T(8,128)(2,1)S(1)}, bf16[80,640]{1,0:T(8,128)(2,1)S(1)}, u32[]{:S(2)}, u32[]{:S(2)}) collective-permute-start(bf16[80,640]{1,0:T(8,128)(2,1)S(1)} %get-tuple-element.118), channel_id=1, source_target_pairs={{0,6},{1,7},{2,0},{3,1},{4,2},{5,3},{6,4},{7,5},{8,14},{9,15},{10,... | collective-permute-start | bytes 307208 | tf_op jit(solution)/shard_map/ppermute | solution.py:29
  128.4 8.6 %collective-permute-start.25 = (bf16[256,640]{1,0:T(8,128)(2,1)S(1)}, bf16[256,640]{1,0:T(8,128)(2,1)S(1)}, u32[]{:S(2)}, u32[]{:S(2)}) collective-permute-start(bf16[256,640]{1,0:T(8,128)(2,1)S(1)} %get-tuple-element.120), channel_id=1, source_target_pairs={{0,2},{1,3},{2,4},{3,5},{4,6},{5,7},{6,0},{7,1},{8,10},{9,11},{10,... | collective-permute-start | bytes 983048 | tf_op jit(solution)/shard_map/ppermute | solution.py:29
  128.5 8.5 %collective-permute-start.26 = (bf16[256,640]{1,0:T(8,128)(2,1)S(1)}, bf16[256,640]{1,0:T(8,128)(2,1)S(1)}, u32[]{:S(2)}, u32[]{:S(2)}) collective-permute-start(bf16[256,640]{1,0:T(8,128)(2,1)S(1)} %get-tuple-element.121), channel_id=1, source_target_pairs={{0,6},{1,7},{2,0},{3,1},{4,2},{5,3},{6,4},{7,5},{8,14},{9,15},{10,... | collective-permute-start | bytes 983048 | tf_op jit(solution)/shard_map/ppermute | solution.py:29
  141.6 7.4 %collective-permute-start.30 = (bf16[256,640]{1,0:T(8,128)(2,1)S(1)}, bf16[256,640]{1,0:T(8,128)(2,1)S(1)}, u32[]{:S(2)}, u32[]{:S(2)}) collective-permute-start(bf16[256,640]{1,0:T(8,128)(2,1)S(1)} %get-tuple-element.125), channel_id=1, source_target_pairs={{0,8},{1,9},{2,10},{3,11},{4,12},{5,13},{6,14},{7,15},{8,0},{9,1},... | collective-permute-start | bytes 983048 | tf_op jit(solution)/shard_map/ppermute | solution.py:29
  149.4 10.5 %collective-permute-start.31 = (bf16[256,320]{1,0:T(8,128)(2,1)S(1)}, bf16[256,320]{1,0:T(8,128)(2,1)S(1)}, u32[]{:S(2)}, u32[]{:S(2)}) collective-permute-start(bf16[256,320]{1,0:T(8,128)(2,1)S(1)} %get-tuple-element.127), channel_id=1, source_target_pairs={{0,1},{1,0},{2,3},{3,2},{4,5},{5,4},{6,7},{7,6},{8,9},{9,8},{10,11... | collective-permute-start | bytes 491528 | tf_op jit(solution)/shard_map/ppermute | solution.py:33
  (50 other events, 293.2 us)

commit v3 on v2

--- a/solution.py
+++ b/solution.py
@@ -165,7 +165,7 @@
 def pick(tokens, rank, table, me, base):
     parts, count = tokens.shape
     features, vocab_rows = table.shape
-    tile, piece = 1280, 256
+    tile, piece = 2432, 128
     steps = pl.cdiv(vocab_rows, tile)
 
     def kernel(me_ref, base_ref, tokens_ref, rank_ref, table_ref, out_ref, list_ref, total_ref):
@@ -258,7 +258,7 @@
     )
 
 
-def embed(tokens, table, me, core, before, beside):
+def embed(tokens, table, me, core, beside):
     rank, most = ranks(tokens, me, table.shape[1])
 
     def more(state):
@@ -269,8 +269,7 @@
         return base + slots, kept + more_kept, passed + more_passed
 
     base = jnp.zeros((), i32)
-    picked = pick(tokens, rank, table, me, base)
-    sent = after(picked, before)
+    sent = pick(tokens, rank, table, me, base)
     got = lax.all_to_all(sent, "rep", 0, 0, tiled=True)
     beside = beside(sent)
     first = place_slots(core, rank, got, base, beside)
@@ -615,7 +614,7 @@
     count, query_width = query.shape
     block_size, head_size = caches[0].shape[1:]
     group = query_width // head_size
-    rows_a_step = 8
+    rows_a_step = 32
     block = rows_a_step * step_count
     half_rows = count // step_count
     grid = half_rows // rows_a_step
@@ -685,7 +684,7 @@
         + [cache_spec] * 4
         + [limit_spec],
         out_specs=rows_spec(query_width),
-        room=10,
+        room=32,
         flops=4 * count * query_width * 2 * 2 * block_size,
     )
 
@@ -877,7 +876,7 @@
 
     tokens = step_token_index.reshape(step_count, replica_count, 2, half_rows)
     tokens = tokens.transpose(1, 2, 3, 0).reshape(replica_count, 2 * count)
-    kept, passed, beside = embed(tokens, embedding.T, me, core, slices_own, beside)
+    kept, passed, beside = embed(tokens, embedding.T, me, core, beside)
     tables, *slices, pairs = beside[:4]
     own, power = to_rows(core, kept, to_partner(passed))
 

time: 162 us -> 159 us (0.981)
  Pallas kernels: 50.3 us -> 46.3 us
    pallas_call x21, Pallas kernels: 50.3 us -> 46.3 us  [call(): pl.pallas_call(kernel, out_shape=out_shape, grid_spec=pltpu.PrefetchScala...]
where the time goes in v3:
time: 159 us; the launch traced here: 158 us
  starting transfers between devices  56.8 us (36%)
  Pallas kernels  46.3 us (29%)
  waiting for transfers between devices  30.1 us (19%)
  local copies, waits for them, and re-layouts  18.9 us (12%)
  other arithmetic  4.39 us (3%)
    pallas_call x21, Pallas kernels, call(): pl.pallas_call(kernel, out_shape=out_shape, grid_spec=pltpu.PrefetchScala...  46.3 us
    ppermute x20, starting transfers between devices, to_tp(): return lax.ppermute(block, 'tp', tp_route(dz, dy, 0))  30.8 us
    unnamed x80, local copies, waits for them, and re-layouts  17.5 us
    ppermute x20, waiting for transfers between devices, to_tp(): return lax.ppermute(block, 'tp', tp_route(dz, dy, 0))  15.2 us
    ppermute x8, starting transfers between devices, to_partner(): return lax.ppermute(block, 'tp', tp_route(0, 0, 1))  13.5 us
    all_to_all x1, starting transfers between devices, over_replicas(): return lax.all_to_all(copies, 'rep', 0, 0, tiled=True)  5.47 us
    all_to_all x1, waiting for transfers between devices, embed(): got = lax.all_to_all(sent, 'rep', 0, 0, tiled=True)  5.12 us
    ppermute x4, waiting for transfers between devices, to_other_side(): return lax.ppermute(value, 'tp', route)  4.92 us
  transfers between devices with their start and end apart: 34, of which 10 were waited for; matrix products, arithmetic and copies ran while one was open for 4% of the time, Pallas kernels for 20%

profile of v3, /device:TPU:1, one launch (start us, length us, event | category | flops | bytes accessed | tf_op | source)
XLA Modules:
  0.0 157.9 jit_solution(12148448955270862780)
XLA Ops:
  5.9 5.5 %all-to-all-start.2 = ((bf16[8,4,16,832]{3,2,1,0:T(8,128)(2,1)}), bf16[8,4,16,832]{3,2,1,0:T(8,128)(2,1)S(1)}, u32[]{:S(2)}, u32[]{:S(2)}) async-start(bf16[8,4,16,832]{3,2,1,0:T(8,128)(2,1)} %broadcast_in_dim.20), calls=%async_computation.2 | async-start | bytes 1835008 | tf_op jit(solution)/shard_map/all_to_all | solution.py:39
  13.1 9.4 %shard_map.164.refs_0_.refs_1_.ready_ref = bf16[8,320,128]{2,1,0:T(8,128)(2,1)S(1)} custom-call(s32[1]{0:T(128)} %bitcast.13.me_ref, s32[1]{0:T(128)} %constant.136.clone.1.base_ref, s32[8,512]{1,0:T(8,128)S(1)} %copy.22.tokens_ref, s32[16,512]{1,0:T(8,128)S(1)} %get-tuple-element.222.rank_ref, bf16[320,9496]{1,0:T(8,128)(2,1)} %bitcast.58), custom_call_target="tpu_custom_call" | custom-call | flops 6223298560 | bytes 6126592 | tf_op jit(solution)/shard_map/pallas_call | solution.py:74
  23.4 2.5 %all-to-all-done.2.refs_0_ = bf16[8,4,16,832]{3,2,1,0:T(8,128)(2,1)S(1)} async-done(((bf16[8,4,16,832]{3,2,1,0:T(8,128)(2,1)}), bf16[8,4,16,832]{3,2,1,0:T(8,128)(2,1)S(1)}, u32[]{:S(2)}, u32[]{:S(2)}) %all-to-all-start.2) | async-done | bytes 852000 | tf_op jit(solution)/shard_map/all_to_all | solution.py:39
  27.7 4.2 %all-to-all-start.1 = ((bf16[8,320,128]{2,1,0:T(8,128)(2,1)}), bf16[8,320,128]{2,1,0:T(8,128)(2,1)}, u32[]{:S(2)}, u32[]{:S(2)}) async-start(bf16[8,320,128]{2,1,0:T(8,128)(2,1)} %copy-done.5), calls=%async_computation.1 | async-start | bytes 1310720 | tf_op jit(solution)/shard_map/all_to_all | solution.py:273
  38.5 5.1 %all-to-all-done.1.got_ref = bf16[8,320,128]{2,1,0:T(8,128)(2,1)} async-done(((bf16[8,320,128]{2,1,0:T(8,128)(2,1)}), bf16[8,320,128]{2,1,0:T(8,128)(2,1)}, u32[]{:S(2)}, u32[]{:S(2)}) %all-to-all-start.1) | async-done | bytes 655392 | tf_op jit(solution)/shard_map/all_to_all | solution.py:273
  44.7 2.7 %shard_map.168 = (bf16[320,256]{1,0:T(8,128)(2,1)}, bf16[320,256]{1,0:T(8,128)(2,1)}) custom-call(s32[1]{0:T(128)} %bitcast.4.core_ref, s32[1]{0:T(128)} %constant.136.clone.1.base_ref, s32[16,512]{1,0:T(8,128)} %copy-done.35, bf16[8,320,128]{2,1,0:T(8,128)(2,1)} %all-to-all-done.1.got_ref, f32[256,384]{1,0:T(8,128)S(1)} %copy-done.9, ...), custom_call_target="tpu_custom_call" | custom-call | flops 1048576 | bytes 22183936 | tf_op jit(solution)/shard_map/pallas_call | solution.py:74
  54.1 3.3 %collective-permute-start.9 = (bf16[256,640]{1,0:T(8,128)(2,1)S(1)}, bf16[256,640]{1,0:T(8,128)(2,1)S(1)}, u32[]{:S(2)}, u32[]{:S(2)}) collective-permute-start(bf16[256,640]{1,0:T(8,128)(2,1)S(1)} %get-tuple-element.97.own_ref.plain_ref), channel_id=1, source_target_pairs={{0,8},{1,9},{2,10},{3,11},{4,12},{5,13},{6,14},{7,15},{8,0},{9,1},... | collective-permute-start | bytes 983048 | tf_op jit(solution)/shard_map/ppermute | solution.py:29
  57.5 7.3 %collective-permute-done.10 = f32[2,128]{1,0:T(2,128)S(1)} collective-permute-done((f32[2,128]{1,0:T(2,128)S(1)}, f32[2,128]{1,0:T(2,128)S(1)}, u32[]{:S(2)}, u32[]{:S(2)}) %collective-permute-start.10) | collective-permute-done | bytes 1056 | tf_op jit(solution)/shard_map/ppermute | solution.py:29
  66.8 2.7 %collective-permute-start.12 = (bf16[256,640]{1,0:T(8,128)(2,1)S(1)}, bf16[256,640]{1,0:T(8,128)(2,1)S(1)}, u32[]{:S(2)}, u32[]{:S(2)}) collective-permute-start(bf16[256,640]{1,0:T(8,128)(2,1)S(1)} %get-tuple-element.100), channel_id=1, source_target_pairs={{0,6},{1,7},{2,0},{3,1},{4,2},{5,3},{6,4},{7,5},{8,14},{9,15},{10,... | collective-permute-start | bytes 983048 | tf_op jit(solution)/shard_map/ppermute | solution.py:29
  69.5 4.9 %collective-permute-done.17 = f32[2,128]{1,0:T(2,128)S(1)} collective-permute-done((f32[2,128]{1,0:T(2,128)}, f32[2,128]{1,0:T(2,128)S(1)}, u32[]{:S(2)}, u32[]{:S(2)}) %collective-permute-start.17) | collective-permute-done | bytes 1056 | tf_op jit(solution)/shard_map/ppermute | solution.py:326
  80.0 2.6 %shard_map.173 = (f32[256,128]{1,0:T(8,128)S(1)}, f32[256,128]{1,0:T(8,128)}) custom-call(s32[1]{0:T(128)} %bitcast.4.core_ref, s32[1]{0:T(128)} %bitcast.22.chip_ref, bf16[256,640]{1,0:T(8,128)(2,1)S(1)} %get-tuple-element.97.own_ref.plain_ref, f32[2,128]{1,0:T(2,128)S(1)} %add.156.power_ref, f32[8,1,640]{2,1,0:T(1,128)S(1)} %bitcast.43, ...), custom_call_target="tpu_custom_call" | custom-call | flops 167772160 | bytes 2548736 | tf_op jit(solution)/shard_map/pallas_call | solution.py:74
  90.6 2.5 %copy-done = bf16[5120,512]{1,0:T(8,128)(2,1)S(1)} copy-done((bf16[5120,512]{1,0:T(8,128)(2,1)S(1)}, bf16[5120,512]{1,0:T(8,128)(2,1)}, u32[]{:S(2)}) %copy-start) | copy-done | bytes 5242904
  96.2 4.9 %shard_map.174 = (f32[256,512]{1,0:T(8,128)S(1)}, f32[256,512]{1,0:T(8,128)S(1)}, f32[256,256]{1,0:T(8,128)S(1)}) custom-call(s32[4]{0:T(128)S(1)} %pad_add_fusion.2.places_ref, bf16[256,2560]{1,0:T(8,128)(2,1)S(1)} %copy-done.17, f32[256,128]{1,0:T(8,128)S(1)} %get-tuple-element.105.refs_1_.refs_6_, f32[8,1,640]{2,1,0:T(1,128)S(1)} %bitcast.44, ...), custom_call_target="tpu_custom_call" | custom-call | flops 1677721600 | bytes 53952512 | tf_op jit(solution)/shard_map/pallas_call | solution.py:74
  102.1 4.9 %shard_map.176 = (f32[256,512]{1,0:T(8,128)S(1)}, f32[256,512]{1,0:T(8,128)S(1)}, f32[256,256]{1,0:T(8,128)S(1)}) custom-call(s32[4]{0:T(128)S(1)} %pad_add_fusion.1.places_ref, bf16[256,640]{1,0:T(8,128)(2,1)S(1)} %collective-permute-done.11.up_ref.refs_0_, bf16[256,640]{1,0:T(8,128)(2,1)S(1)} %collective-permute-done.12.down_ref.refs_1_, ...), custom_call_target="tpu_custom_call" | custom-call | flops 1677721600 | bytes 55394304 | tf_op jit(solution)/shard_map/pallas_call | solution.py:74
  107.1 2.8 %shard_map.177 = (f32[256,1024]{1,0:T(8,128)S(1)}, bf16[256,128]{1,0:T(8,128)(2,1)S(1)}, bf16[256,128]{1,0:T(8,128)(2,1)S(1)}) custom-call(s32[1]{0:T(128)} %bitcast.4.core_ref, f32[256,512]{1,0:T(8,128)S(1)} %get-tuple-element.111.own_ref, f32[256,512]{1,0:T(8,128)S(1)} %get-tuple-element.112.other_ref, f32[256,256]{1,0:T(8,128)S(1)} %get-tuple-element.113.kv_ref, ...), custom_call_target="tpu_custom_call" | custom-call | flops 2147483648 | bytes 3671040 | tf_op jit(solution)/shard_map/pallas_call | solution.py:74
  109.9 4.5 %shard_map.178.attended_ref = bf16[256,1024]{1,0:T(8,128)(2,1)S(1)} custom-call(s32[1]{0:T(128)} %bitcast.4.core_ref, s32[128]{0:T(128)S(1)} %copy-done.24, f32[256,1024]{1,0:T(8,128)S(1)} %get-tuple-element.114.query_ref, bf16[256,128]{1,0:T(8,128)(2,1)S(1)} %get-tuple-element.115.new_key_ref, bf16[256,128]{1,0:T(8,128)(2,1)S(1)} %get-tuple-element.116.new_value_ref, ...), custom_call_target="tpu_custom_call" | custom-call | flops 402653184 | bytes 14172160 | tf_op jit(solution)/shard_map/pallas_call | solution.py:74
  119.0 2.5 %collective-permute-start.24 = (bf16[96,640]{1,0:T(8,128)(2,1)S(1)}, bf16[96,640]{1,0:T(8,128)(2,1)S(1)}, u32[]{:S(2)}, u32[]{:S(2)}) collective-permute-start(bf16[96,640]{1,0:T(8,128)(2,1)S(1)} %get-tuple-element.119), channel_id=1, source_target_pairs={{0,8},{1,9},{2,10},{3,11},{4,12},{5,13},{6,14},{7,15},{8,0},{9,1},... | collective-permute-start | bytes 368648 | tf_op jit(solution)/shard_map/ppermute | solution.py:29
  121.6 3.5 %shard_map.180.blocks_ref = bf16[3,256,640]{2,1,0:T(8,128)(2,1)S(1)} custom-call(s32[3]{0:T(128)S(1)} %pad_add_fusion.3.places_ref, bf16[256,1024]{1,0:T(8,128)(2,1)S(1)} %shard_map.178.attended_ref, bf16[512,5120]{1,0:T(8,128)(2,1)S(1)} %bitcast.38, bf16[512,5120]{1,0:T(8,128)(2,1)} %collective-permute-done.5.refs_7_.other_ref), custom_call_target="tpu_custom_call" | custom-call | flops 1006632960 | bytes 11010048 | tf_op jit(solution)/shard_map/pallas_call | solution.py:74
  125.3 2.7 %collective-permute-start.26 = (bf16[256,640]{1,0:T(8,128)(2,1)S(1)}, bf16[256,640]{1,0:T(8,128)(2,1)S(1)}, u32[]{:S(2)}, u32[]{:S(2)}) collective-permute-start(bf16[256,640]{1,0:T(8,128)(2,1)S(1)} %get-tuple-element.121), channel_id=1, source_target_pairs={{0,6},{1,7},{2,0},{3,1},{4,2},{5,3},{6,4},{7,5},{8,14},{9,15},{10,... | collective-permute-start | bytes 983048 | tf_op jit(solution)/shard_map/ppermute | solution.py:29
  129.7 4.1 %shard_map.179.blocks_ref = bf16[4,256,640]{2,1,0:T(8,128)(2,1)S(1)} custom-call(s32[4]{0:T(128)S(1)} %pad_add_fusion.places_ref, bf16[256,1024]{1,0:T(8,128)(2,1)S(1)} %shard_map.178.attended_ref, bf16[512,5120]{1,0:T(8,128)(2,1)S(1)} %bitcast.38, bf16[512,5120]{1,0:T(8,128)(2,1)} %collective-permute-done.5.refs_7_.other_ref), custom_call_target="tpu_custom_call" | custom-call | flops 1342177280 | bytes 11010048 | tf_op jit(solution)/shard_map/pallas_call | solution.py:74
  135.7 2.7 %collective-permute-start.29 = (bf16[256,640]{1,0:T(8,128)(2,1)S(1)}, bf16[256,640]{1,0:T(8,128)(2,1)S(1)}, u32[]{:S(2)}, u32[]{:S(2)}) collective-permute-start(bf16[256,640]{1,0:T(8,128)(2,1)S(1)} %get-tuple-element.124), channel_id=1, source_target_pairs={{0,6},{1,7},{2,0},{3,1},{4,2},{5,3},{6,4},{7,5},{8,14},{9,15},{10,... | collective-permute-start | bytes 983048 | tf_op jit(solution)/shard_map/ppermute | solution.py:29
  140.0 2.9 %collective-permute-done.28.up_ref = bf16[256,640]{1,0:T(8,128)(2,1)S(1)} collective-permute-done((bf16[256,640]{1,0:T(8,128)(2,1)S(1)}, bf16[256,640]{1,0:T(8,128)(2,1)S(1)}, u32[]{:S(2)}, u32[]{:S(2)}) %collective-permute-start.28) | collective-permute-done | bytes 327712 | tf_op jit(solution)/shard_map/ppermute | solution.py:29
  142.9 3.0 %collective-permute-done.30.over_ref = bf16[256,640]{1,0:T(8,128)(2,1)S(1)} collective-permute-done((bf16[256,640]{1,0:T(8,128)(2,1)S(1)}, bf16[256,640]{1,0:T(8,128)(2,1)S(1)}, u32[]{:S(2)}, u32[]{:S(2)}) %collective-permute-start.30) | collective-permute-done | bytes 327712 | tf_op jit(solution)/shard_map/ppermute | solution.py:29
  146.2 9.4 %collective-permute-start.31 = (bf16[256,320]{1,0:T(8,128)(2,1)S(1)}, bf16[256,320]{1,0:T(8,128)(2,1)S(1)}, u32[]{:S(2)}, u32[]{:S(2)}) collective-permute-start(bf16[256,320]{1,0:T(8,128)(2,1)S(1)} %get-tuple-element.127), channel_id=1, source_target_pairs={{0,1},{1,0},{2,3},{3,2},{4,5},{5,4},{6,7},{7,6},{8,9},{9,8},{10,11... | collective-permute-start | bytes 491528 | tf_op jit(solution)/shard_map/ppermute | solution.py:33
  (164 shorter events, 56.8 us)
Async XLA Ops:
  0.0 43.6 %collective-permute-start.2 = (bf16[5120,512]{1,0:T(8,128)(2,1)}, bf16[5120,512]{1,0:T(8,128)(2,1)}, u32[]{:S(2)}, u32[]{:S(2)}) collective-permute-start(bf16[5120,512]{1,0:T(8,128)(2,1)} %refs_14_.1), channel_id=1, source_target_pairs={{0,1},{1,0},{2,3},{3,2},{4,5},{5,4},{6,7},{7,6},{8,9},{9,8},{10,11... | collective-permute-start | bytes 15728648 | tf_op jit(solution)/shard_map/ppermute | solution.py:33
  1.4 42.2 %collective-permute-start.5 = (bf16[512,5120]{1,0:T(8,128)(2,1)}, bf16[512,5120]{1,0:T(8,128)(2,1)}, u32[]{:S(2)}, u32[]{:S(2)}) collective-permute-start(bf16[512,5120]{1,0:T(8,128)(2,1)} %own_ref.5), channel_id=1, source_target_pairs={{0,1},{1,0},{2,3},{3,2},{4,5},{5,4},{6,7},{7,6},{8,9},{9,8},{10,11... | collective-permute-start | bytes 15728648 | tf_op jit(solution)/shard_map/ppermute | solution.py:33
  1.4 42.2 %collective-permute-start.3 = (bf16[128,96,128]{2,1,0:T(8,128)(2,1)}, bf16[128,96,128]{2,1,0:T(8,128)(2,1)}, u32[]{:S(2)}, u32[]{:S(2)}) collective-permute-start(bf16[128,96,128]{2,1,0:T(8,128)(2,1)} %own_key_ref.1), channel_id=1, source_target_pairs={{0,1},{1,0},{2,3},{3,2},{4,5},{5,4},{6,7},{7,6},{8,9},{9,8},{10,11... | collective-permute-start | bytes 9437192 | tf_op jit(solution)/shard_map/ppermute | solution.py:33
  1.9 41.7 %collective-permute-start.4 = (bf16[128,96,128]{2,1,0:T(8,128)(2,1)}, bf16[128,96,128]{2,1,0:T(8,128)(2,1)}, u32[]{:S(2)}, u32[]{:S(2)}) collective-permute-start(bf16[128,96,128]{2,1,0:T(8,128)(2,1)} %own_value_ref.1), channel_id=1, source_target_pairs={{0,1},{1,0},{2,3},{3,2},{4,5},{5,4},{6,7},{7,6},{8,9},{9,8},{10,11... | collective-permute-start | bytes 9437192 | tf_op jit(solution)/shard_map/ppermute | solution.py:33
  4.4 22.5 %collective-permute-start.1 = (bf16[128,5120]{1,0:T(8,128)(2,1)}, bf16[128,5120]{1,0:T(8,128)(2,1)S(1)}, u32[]{:S(2)}, u32[]{:S(2)}) collective-permute-start(bf16[128,5120]{1,0:T(8,128)(2,1)} %pad_maximum_fusion), channel_id=1, source_target_pairs={{0,1},{1,0},{2,3},{3,2},{4,5},{5,4},{6,7},{7,6},{8,9},{9,8},{10,11... | collective-permute-start | bytes 3932168 | tf_op jit(solution)/shard_map/ppermute | solution.py:33
  5.9 20.0 %all-to-all-start.2 = ((bf16[8,4,16,832]{3,2,1,0:T(8,128)(2,1)}), bf16[8,4,16,832]{3,2,1,0:T(8,128)(2,1)S(1)}, u32[]{:S(2)}, u32[]{:S(2)}) async-start(bf16[8,4,16,832]{3,2,1,0:T(8,128)(2,1)} %broadcast_in_dim.20), calls=%async_computation.2 | async-start | bytes 1835008 | tf_op jit(solution)/shard_map/all_to_all | solution.py:39
  26.9 16.8 %collective-permute-start = (bf16[8,4,16,832]{3,2,1,0:T(8,128)(2,1)}, bf16[8,4,16,832]{3,2,1,0:T(8,128)(2,1)}, u32[]{:S(2)}, u32[]{:S(2)}) collective-permute-start(bf16[8,4,16,832]{3,2,1,0:T(8,128)(2,1)} %shard_map.166.refs_1_.own_ref.refs_2_), channel_id=1, source_target_pairs={{0,1},{1,0},{2,3},{3,2},{4,5},{5,4},{6,7},{7,6},{8,9},{9,8},{10,11... | collective-permute-start | bytes 2555912 | tf_op jit(solution)/shard_map/ppermute | solution.py:33
  27.7 15.9 %all-to-all-start.1 = ((bf16[8,320,128]{2,1,0:T(8,128)(2,1)}), bf16[8,320,128]{2,1,0:T(8,128)(2,1)}, u32[]{:S(2)}, u32[]{:S(2)}) async-start(bf16[8,320,128]{2,1,0:T(8,128)(2,1)} %copy-done.5), calls=%async_computation.1 | async-start | bytes 1310720 | tf_op jit(solution)/shard_map/all_to_all | solution.py:273
  51.2 13.5 %collective-permute-start.7 = (bf16[256,640]{1,0:T(8,128)(2,1)S(1)}, bf16[256,640]{1,0:T(8,128)(2,1)S(1)}, u32[]{:S(2)}, u32[]{:S(2)}) collective-permute-start(bf16[256,640]{1,0:T(8,128)(2,1)S(1)} %get-tuple-element.97.own_ref.plain_ref), channel_id=1, source_target_pairs={{0,2},{1,3},{2,4},{3,5},{4,6},{5,7},{6,0},{7,1},{8,10},{9,11},{10,... | collective-permute-start | bytes 983048 | tf_op jit(solution)/shard_map/ppermute | solution.py:29
  52.6 12.2 %collective-permute-start.8 = (bf16[256,640]{1,0:T(8,128)(2,1)S(1)}, bf16[256,640]{1,0:T(8,128)(2,1)S(1)}, u32[]{:S(2)}, u32[]{:S(2)}) collective-permute-start(bf16[256,640]{1,0:T(8,128)(2,1)S(1)} %get-tuple-element.97.own_ref.plain_ref), channel_id=1, source_target_pairs={{0,6},{1,7},{2,0},{3,1},{4,2},{5,3},{6,4},{7,5},{8,14},{9,15},{10,... | collective-permute-start | bytes 983048 | tf_op jit(solution)/shard_map/ppermute | solution.py:29
  54.1 10.6 %collective-permute-start.9 = (bf16[256,640]{1,0:T(8,128)(2,1)S(1)}, bf16[256,640]{1,0:T(8,128)(2,1)S(1)}, u32[]{:S(2)}, u32[]{:S(2)}) collective-permute-start(bf16[256,640]{1,0:T(8,128)(2,1)S(1)} %get-tuple-element.97.own_ref.plain_ref), channel_id=1, source_target_pairs={{0,8},{1,9},{2,10},{3,11},{4,12},{5,13},{6,14},{7,15},{8,0},{9,1},... | collective-permute-start | bytes 983048 | tf_op jit(solution)/shard_map/ppermute | solution.py:29
  66.8 11.9 %collective-permute-start.11 = (bf16[256,640]{1,0:T(8,128)(2,1)S(1)}, bf16[256,640]{1,0:T(8,128)(2,1)S(1)}, u32[]{:S(2)}, u32[]{:S(2)}) collective-permute-start(bf16[256,640]{1,0:T(8,128)(2,1)S(1)} %get-tuple-element.99), channel_id=1, source_target_pairs={{0,2},{1,3},{2,4},{3,5},{4,6},{5,7},{6,0},{7,1},{8,10},{9,11},{10,... | collective-permute-start | bytes 983048 | tf_op jit(solution)/shard_map/ppermute | solution.py:29
  66.8 11.9 %collective-permute-start.12 = (bf16[256,640]{1,0:T(8,128)(2,1)S(1)}, bf16[256,640]{1,0:T(8,128)(2,1)S(1)}, u32[]{:S(2)}, u32[]{:S(2)}) collective-permute-start(bf16[256,640]{1,0:T(8,128)(2,1)S(1)} %get-tuple-element.100), channel_id=1, source_target_pairs={{0,6},{1,7},{2,0},{3,1},{4,2},{5,3},{6,4},{7,5},{8,14},{9,15},{10,... | collective-permute-start | bytes 983048 | tf_op jit(solution)/shard_map/ppermute | solution.py:29
  76.3 25.7 %collective-permute-start.13 = (bf16[256,640]{1,0:T(8,128)(2,1)}, bf16[256,640]{1,0:T(8,128)(2,1)}, u32[]{:S(2)}, u32[]{:S(2)}) collective-permute-start(bf16[256,640]{1,0:T(8,128)(2,1)} %copy-done.21), channel_id=1, source_target_pairs={{0,8},{1,9},{2,10},{3,11},{4,12},{5,13},{6,14},{7,15},{8,0},{9,1},... | collective-permute-start | bytes 983048 | tf_op jit(solution)/shard_map/ppermute | solution.py:29
  85.2 16.9 %collective-permute-start.15 = (bf16[80,640]{1,0:T(8,128)(2,1)}, bf16[80,640]{1,0:T(8,128)(2,1)S(1)}, u32[]{:S(2)}, u32[]{:S(2)}) collective-permute-start(bf16[80,640]{1,0:T(8,128)(2,1)} %copy-done.22), channel_id=1, source_target_pairs={{0,8},{1,9},{2,10},{3,11},{4,12},{5,13},{6,14},{7,15},{8,0},{9,1},... | collective-permute-start | bytes 307208 | tf_op jit(solution)/shard_map/ppermute | solution.py:29
  85.8 16.2 %collective-permute-start.14 = (bf16[80,640]{1,0:T(8,128)(2,1)}, bf16[80,640]{1,0:T(8,128)(2,1)S(1)}, u32[]{:S(2)}, u32[]{:S(2)}) collective-permute-start(bf16[80,640]{1,0:T(8,128)(2,1)} %copy-done.28), channel_id=1, source_target_pairs={{0,2},{1,3},{2,4},{3,5},{4,6},{5,7},{6,0},{7,1},{8,10},{9,11},{10,... | collective-permute-start | bytes 307208 | tf_op jit(solution)/shard_map/ppermute | solution.py:29
  86.4 15.6 %collective-permute-start.16 = (bf16[96,640]{1,0:T(8,128)(2,1)}, bf16[96,640]{1,0:T(8,128)(2,1)S(1)}, u32[]{:S(2)}, u32[]{:S(2)}) collective-permute-start(bf16[96,640]{1,0:T(8,128)(2,1)} %copy-done.27), channel_id=1, source_target_pairs={{0,6},{1,7},{2,0},{3,1},{4,2},{5,3},{6,4},{7,5},{8,14},{9,15},{10,... | collective-permute-start | bytes 368648 | tf_op jit(solution)/shard_map/ppermute | solution.py:29
  89.9 11.2 %collective-permute-start.20 = (f32[256,128]{1,0:T(8,128)S(1)}, f32[256,128]{1,0:T(8,128)S(1)}, u32[]{:S(2)}, u32[]{:S(2)}) collective-permute-start(f32[256,128]{1,0:T(8,128)S(1)} %add.157.value_ref), channel_id=1, source_target_pairs={{0,2},{1,3},{2,0},{3,1},{4,6},{5,7},{6,4},{7,5},{8,10},{9,11},{10,... | collective-permute-start | bytes 393224 | tf_op jit(solution)/shard_map/ppermute | solution.py:326
  116.3 8.8 %collective-permute-start.22 = (bf16[80,640]{1,0:T(8,128)(2,1)S(1)}, bf16[80,640]{1,0:T(8,128)(2,1)S(1)}, u32[]{:S(2)}, u32[]{:S(2)}) collective-permute-start(bf16[80,640]{1,0:T(8,128)(2,1)S(1)} %get-tuple-element.117), channel_id=1, source_target_pairs={{0,2},{1,3},{2,4},{3,5},{4,6},{5,7},{6,0},{7,1},{8,10},{9,11},{10,... | collective-permute-start | bytes 307208 | tf_op jit(solution)/shard_map/ppermute | solution.py:29
  117.2 7.9 %collective-permute-start.23 = (bf16[80,640]{1,0:T(8,128)(2,1)S(1)}, bf16[80,640]{1,0:T(8,128)(2,1)S(1)}, u32[]{:S(2)}, u32[]{:S(2)}) collective-permute-start(bf16[80,640]{1,0:T(8,128)(2,1)S(1)} %get-tuple-element.118), channel_id=1, source_target_pairs={{0,6},{1,7},{2,0},{3,1},{4,2},{5,3},{6,4},{7,5},{8,14},{9,15},{10,... | collective-permute-start | bytes 307208 | tf_op jit(solution)/shard_map/ppermute | solution.py:29
  125.2 8.5 %collective-permute-start.25 = (bf16[256,640]{1,0:T(8,128)(2,1)S(1)}, bf16[256,640]{1,0:T(8,128)(2,1)S(1)}, u32[]{:S(2)}, u32[]{:S(2)}) collective-permute-start(bf16[256,640]{1,0:T(8,128)(2,1)S(1)} %get-tuple-element.120), channel_id=1, source_target_pairs={{0,2},{1,3},{2,4},{3,5},{4,6},{5,7},{6,0},{7,1},{8,10},{9,11},{10,... | collective-permute-start | bytes 983048 | tf_op jit(solution)/shard_map/ppermute | solution.py:29
  125.3 8.5 %collective-permute-start.26 = (bf16[256,640]{1,0:T(8,128)(2,1)S(1)}, bf16[256,640]{1,0:T(8,128)(2,1)S(1)}, u32[]{:S(2)}, u32[]{:S(2)}) collective-permute-start(bf16[256,640]{1,0:T(8,128)(2,1)S(1)} %get-tuple-element.121), channel_id=1, source_target_pairs={{0,6},{1,7},{2,0},{3,1},{4,2},{5,3},{6,4},{7,5},{8,14},{9,15},{10,... | collective-permute-start | bytes 983048 | tf_op jit(solution)/shard_map/ppermute | solution.py:29
  128.0 7.4 %collective-permute-start.27 = (bf16[256,640]{1,0:T(8,128)(2,1)S(1)}, bf16[256,640]{1,0:T(8,128)(2,1)S(1)}, u32[]{:S(2)}, u32[]{:S(2)}) collective-permute-start(bf16[256,640]{1,0:T(8,128)(2,1)S(1)} %get-tuple-element.122), channel_id=1, source_target_pairs={{0,8},{1,9},{2,10},{3,11},{4,12},{5,13},{6,14},{7,15},{8,0},{9,1},... | collective-permute-start | bytes 983048 | tf_op jit(solution)/shard_map/ppermute | solution.py:29
  146.2 10.5 %collective-permute-start.31 = (bf16[256,320]{1,0:T(8,128)(2,1)S(1)}, bf16[256,320]{1,0:T(8,128)(2,1)S(1)}, u32[]{:S(2)}, u32[]{:S(2)}) collective-permute-start(bf16[256,320]{1,0:T(8,128)(2,1)S(1)} %get-tuple-element.127), channel_id=1, source_target_pairs={{0,1},{1,0},{2,3},{3,2},{4,5},{5,4},{6,7},{7,6},{8,9},{9,8},{10,11... | collective-permute-start | bytes 491528 | tf_op jit(solution)/shard_map/ppermute | solution.py:33
  (50 other events, 288.5 us)
